TPU v7x, 32 devices: a whole 2x2x4 slice. The times are simulated.
32 devices in a mesh: ctx: 8 (over y, x, core), head: 4 (over z).
Axes of the slice: x: 2, y: 2, z: 4, core: 2. Of those that a mesh axis runs over, the one named last changes fastest.
Arguments:
- join_states: bfloat16 [2048, 4096], P('ctx'), may hold values from -6 to 6
- query_weight: bfloat16 [4096, 4096], P(None, 'head'), may hold values from -0.09375 to 0.09375
- out_weight: bfloat16 [4096, 4096], P('head'), may hold values from -0.5 to 0.5
- outline_keys: bfloat16 [8, 4096, 128], P(None, 'ctx'), may hold values from -180 to 180
- outline_values: bfloat16 [8, 4096, 128], P(None, 'ctx'), may hold values from -6 to 6
- branch_keys: bfloat16 [8, 8192, 128], P(None, 'ctx'), may hold values from -6 to 6
- branch_values: bfloat16 [8, 8192, 128], P(None, 'ctx'), may hold values from -6 to 6
- branch_lengths: int32 [8], replicated, may hold values from 0 to 1024, as said below
- visibility: int32 [64, 8], replicated, may hold values 0 or 1
Outputs:
- attention_out: bfloat16 [2048, 4096], P('ctx', 'head')
Inputs may be any that keep to these rules, and one draw needn't show every extreme that they name: `branch_lengths`: exactly one branch in each draw has 1024 live positions.
All inputs are finite; a program needn't handle non-finite values.
Results may differ from a plain program's by a relative error of at most 0.025.
Values may be sent and summed in bfloat16 or wider, within the bound.
A program may use at most 128 MiB of HBM per device.

v0:
```python
import jax
import jax.numpy as jnp
from jax import lax
from jax.sharding import PartitionSpec as P

JSPAN = 32


ROPE_BASE = 500000.0
NEG_FILL = -1e30


def shifted(block, axis, distance):
    devices = range(lax.axis_size(axis))
    route = [((i - distance) % len(devices), i) for i in devices]
    return lax.ppermute(block, axis, route)


def rope(queries, first):
    rows = queries.shape[0]
    width = queries.shape[-1]
    half = width // 2
    freq = ROPE_BASE ** (-(jnp.arange(half, dtype=jnp.float32) * 2.0) / width)
    place = (first + jnp.arange(rows)).astype(jnp.float32)
    angle = place[:, None, None] * freq[None, None, :]
    cosine = jnp.cos(angle)
    sine = jnp.sin(angle)
    lower = queries[..., :half]
    upper = queries[..., half:]
    return jnp.concatenate([lower * cosine - upper * sine, upper * cosine + lower * sine], axis=-1)


def block_scores(query, keys, visible, scale):
    scores = jnp.einsum("rkgd,ktd->rkgt", query, keys, preferred_element_type=jnp.float32) * scale
    return jnp.where(visible[:, None, None, :], scores, NEG_FILL)


def body(
    join_states,
    query_weight,
    out_weight,
    outline_keys,
    outline_values,
    branch_keys,
    branch_values,
    branch_lengths,
    visibility,
):
    width = outline_keys.shape[2]
    head_count = query_weight.shape[1] // width
    kv_total = outline_keys.shape[0]
    group = head_count * lax.axis_size("head") // kv_total
    kv_local = max(1, head_count // group)
    per_kv = head_count // kv_local
    kv_start = lax.axis_index("head") * head_count // group
    rows = join_states.shape[0]
    n_ctx = lax.axis_size("ctx")
    me = lax.axis_index("ctx")
    outline_here = outline_keys.shape[1]
    branch_most = branch_keys.shape[1]
    scale = width ** (-0.5)
    queries = jnp.dot(join_states, query_weight, preferred_element_type=jnp.float32).reshape(
        rows, head_count, width
    )
    rotated = rope(queries, outline_here * n_ctx + branch_most + me * rows).astype(jnp.bfloat16)
    rotated = rotated.reshape(rows, kv_local, per_kv, width)
    keys = jnp.concatenate(
        [
            lax.dynamic_slice_in_dim(outline_keys, kv_start, kv_local, 0),
            lax.dynamic_slice_in_dim(branch_keys, kv_start, kv_local, 0),
        ],
        axis=1,
    )
    values = jnp.concatenate(
        [
            lax.dynamic_slice_in_dim(outline_values, kv_start, kv_local, 0),
            lax.dynamic_slice_in_dim(branch_values, kv_start, kv_local, 0),
        ],
        axis=1,
    )

    def visible_for(source, row_start, count):
        column = lax.dynamic_index_in_dim(visibility, source, 1, keepdims=False)
        row_flags = lax.dynamic_slice_in_dim(jnp.repeat(column, JSPAN), row_start, count)
        length = lax.dynamic_index_in_dim(branch_lengths, source, 0, keepdims=False)
        branch_part = (row_flags[:, None] == 1) & (jnp.arange(branch_most)[None, :] < length)
        return jnp.concatenate([jnp.ones((count, outline_here), dtype=bool), branch_part], axis=1)

    def absorb(state, pair, visible):
        best, total, acc = state
        scores = block_scores(rotated, pair[0], visible, scale)
        new_best = jnp.maximum(best, jnp.max(scores, axis=-1))
        factor = jnp.exp(best - new_best)
        weights = jnp.where(visible[:, None, None, :], jnp.exp(scores - new_best[..., None]), 0.0)
        total = total * factor + jnp.sum(weights, axis=-1)
        acc = acc * factor[..., None] + jnp.einsum(
            "rkgt,ktd->rkgd",
            weights.astype(jnp.bfloat16),
            pair[1],
            preferred_element_type=jnp.float32,
        )
        return (new_best, total, acc)

    start_state = (
        jnp.full((rows, kv_local, per_kv), NEG_FILL, jnp.float32),
        jnp.zeros((rows, kv_local, per_kv), jnp.float32),
        jnp.zeros((rows, kv_local, per_kv, width), jnp.float32),
    )

    def turn(step, carry):
        pair, state = carry
        state = absorb(state, pair, visible_for((me - step) % n_ctx, me * rows, rows))
        pair = shifted(pair, "ctx", 1)
        return (pair, state)

    pair, state = lax.fori_loop(0, n_ctx - 1, turn, (jnp.stack([keys, values]), start_state))
    state = absorb(state, pair, visible_for((me - n_ctx + 1) % n_ctx, me * rows, rows))
    mixed = state[2] / state[1][..., None]
    mixed = mixed.astype(jnp.bfloat16).reshape(rows, head_count * width)
    partial_out = jnp.dot(mixed, out_weight, preferred_element_type=jnp.float32)
    return lax.psum_scatter(
        partial_out.astype(jnp.bfloat16), "head", scatter_dimension=1, tiled=True
    )


def solution(mesh):
    return jax.shard_map(
        body,
        mesh=mesh,
        in_specs=(
            P("ctx", None),
            P(None, "head"),
            P("head", None),
            P(None, "ctx", None),
            P(None, "ctx", None),
            P(None, "ctx", None),
            P(None, "ctx", None),
            P(),
            P(),
        ),
        out_specs=P("ctx", "head"),
        check_vma=False,
    )
```

profile of v0, /device:TPU:0, one launch (start us, length us, event | category | flops | bytes accessed | tf_op | source)
XLA Modules:
  0.0 273.3 jit_solution(11455188285783930408)
XLA Ops:
  8.1 5.7 %convolution_bitcast_fusion = f32[32,8,8,128]{3,1,2,0:T(8,128)S(1)} fusion(bf16[256,4096]{1,0:T(8,128)(2,1)S(1)} %copy-done, bf16[4096,1024]{1,0:T(8,128)(2,1)} %param.12), kind=kOutput, calls=%fused_computation.36 | convolution fusion | flops 2147483648 | bytes 11534336 | tf_op jit(solution)/shard_map/dot_general | solution.py:62
  22.0 170.1 %while.22 = (s32[]{:T(128)}, bf16[2,2,1536,128]{3,2,1,0:T(8,128)(2,1)}, f32[256,2,4]{0,2,1:T(4,128)S(1)}, f32[256,2,4]{0,2,1:T(4,128)S(1)}, f32[256,2,4,128]{3,0...) while((s32[]{:T(128)}, ...), condition=%wide.region_3.4_spmd.clone, body=%wide.region_0.3_spmd.clone.sunk | while | flops 1652567296 | bytes 103969416 | solution.py:116
  28.7 4.5 %copy-done.2 = f32[2,1536,256,4]{2,1,3,0:T(8,128)} copy-done((f32[2,1536,256,4]{2,1,3,0:T(8,128)}, f32[2,1536,256,4]{2,1,3,0:T(8,128)S(1)}, u32[]{:S(2)}) %copy-start.2) | copy-done | bytes 12582936 | tf_op jit(solution)/shard_map/while
  33.2 3.0 %fusion.59 = f32[256,2,4]{0,2,1:T(4,128)S(1)} fusion(f32[2,1536,256,4]{2,1,3,0:T(8,128)S(1)} %get-tuple-element.379, f32[256,2,4]{0,2,1:T(4,128)S(1)} %select_maximum_fusion.2, pred[256,1536]{0,1:T(8,128)(4,1)S(1)} %concatenate.31), kind=kLoop, calls=%fused_computation.4.clone.1 | loop fusion | flops 15726592 | bytes 12992512 | tf_op jit(solution)/shard_map/while/body/eval_jaxpr/reduce_sum | solution.py:95
  36.3 9.5 %fusion.61 = f32[256,2,4,128]{3,0,2,1:T(8,128)} fusion(f32[2,1536,256,4]{2,1,3,0:T(8,128)} %copy-done.2, f32[256,2,4]{0,2,1:T(4,128)S(1)} %select_maximum_fusion.2, pred[256,1536]{0,1:T(8,128)(4,1)S(1)} %concatenate.31, f32[256,2,4,128]{3,0,2,1:T(8,128)} %get-tuple-element.401, bf16[2,2,1536,128]{3,2,1,0:T(8,128)(2,1)S(1)} %copy.35, ...), kind=kOutput, calls=%fused_computation.8.clone.1 | convolution fusion | flops 821821440 | bytes 15876097 | tf_op jit(solution)/shard_map/while/body/eval_jaxpr/rkgt,ktd->rkgd/dot_general | solution.py:96
  54.5 4.5 %copy-done.2 = f32[2,1536,256,4]{2,1,3,0:T(8,128)} copy-done((f32[2,1536,256,4]{2,1,3,0:T(8,128)}, f32[2,1536,256,4]{2,1,3,0:T(8,128)S(1)}, u32[]{:S(2)}) %copy-start.2) | copy-done | bytes 12582936 | tf_op jit(solution)/shard_map/while
  59.0 3.0 %fusion.59 = f32[256,2,4]{0,2,1:T(4,128)S(1)} fusion(f32[2,1536,256,4]{2,1,3,0:T(8,128)S(1)} %get-tuple-element.379, f32[256,2,4]{0,2,1:T(4,128)S(1)} %select_maximum_fusion.2, pred[256,1536]{0,1:T(8,128)(4,1)S(1)} %concatenate.31), kind=kLoop, calls=%fused_computation.4.clone.1 | loop fusion | flops 15726592 | bytes 12992512 | tf_op jit(solution)/shard_map/while/body/eval_jaxpr/reduce_sum | solution.py:95
  62.1 9.7 %fusion.61 = f32[256,2,4,128]{3,0,2,1:T(8,128)} fusion(f32[2,1536,256,4]{2,1,3,0:T(8,128)} %copy-done.2, f32[256,2,4]{0,2,1:T(4,128)S(1)} %select_maximum_fusion.2, pred[256,1536]{0,1:T(8,128)(4,1)S(1)} %concatenate.31, f32[256,2,4,128]{3,0,2,1:T(8,128)} %get-tuple-element.401, bf16[2,2,1536,128]{3,2,1,0:T(8,128)(2,1)S(1)} %copy.35, ...), kind=kOutput, calls=%fused_computation.8.clone.1 | convolution fusion | flops 821821440 | bytes 15876097 | tf_op jit(solution)/shard_map/while/body/eval_jaxpr/rkgt,ktd->rkgd/dot_general | solution.py:96
  77.9 4.5 %copy-done.2 = f32[2,1536,256,4]{2,1,3,0:T(8,128)} copy-done((f32[2,1536,256,4]{2,1,3,0:T(8,128)}, f32[2,1536,256,4]{2,1,3,0:T(8,128)S(1)}, u32[]{:S(2)}) %copy-start.2) | copy-done | bytes 12582936 | tf_op jit(solution)/shard_map/while
  85.5 9.7 %fusion.61 = f32[256,2,4,128]{3,0,2,1:T(8,128)} fusion(f32[2,1536,256,4]{2,1,3,0:T(8,128)} %copy-done.2, f32[256,2,4]{0,2,1:T(4,128)S(1)} %select_maximum_fusion.2, pred[256,1536]{0,1:T(8,128)(4,1)S(1)} %concatenate.31, f32[256,2,4,128]{3,0,2,1:T(8,128)} %get-tuple-element.401, bf16[2,2,1536,128]{3,2,1,0:T(8,128)(2,1)S(1)} %copy.35, ...), kind=kOutput, calls=%fused_computation.8.clone.1 | convolution fusion | flops 821821440 | bytes 15876097 | tf_op jit(solution)/shard_map/while/body/eval_jaxpr/rkgt,ktd->rkgd/dot_general | solution.py:96
  102.9 4.5 %copy-done.2 = f32[2,1536,256,4]{2,1,3,0:T(8,128)} copy-done((f32[2,1536,256,4]{2,1,3,0:T(8,128)}, f32[2,1536,256,4]{2,1,3,0:T(8,128)S(1)}, u32[]{:S(2)}) %copy-start.2) | copy-done | bytes 12582936 | tf_op jit(solution)/shard_map/while
  107.4 3.0 %fusion.59 = f32[256,2,4]{0,2,1:T(4,128)S(1)} fusion(f32[2,1536,256,4]{2,1,3,0:T(8,128)S(1)} %get-tuple-element.379, f32[256,2,4]{0,2,1:T(4,128)S(1)} %select_maximum_fusion.2, pred[256,1536]{0,1:T(8,128)(4,1)S(1)} %concatenate.31), kind=kLoop, calls=%fused_computation.4.clone.1 | loop fusion | flops 15726592 | bytes 12992512 | tf_op jit(solution)/shard_map/while/body/eval_jaxpr/reduce_sum | solution.py:95
  110.5 9.7 %fusion.61 = f32[256,2,4,128]{3,0,2,1:T(8,128)} fusion(f32[2,1536,256,4]{2,1,3,0:T(8,128)} %copy-done.2, f32[256,2,4]{0,2,1:T(4,128)S(1)} %select_maximum_fusion.2, pred[256,1536]{0,1:T(8,128)(4,1)S(1)} %concatenate.31, f32[256,2,4,128]{3,0,2,1:T(8,128)} %get-tuple-element.401, bf16[2,2,1536,128]{3,2,1,0:T(8,128)(2,1)S(1)} %copy.35, ...), kind=kOutput, calls=%fused_computation.8.clone.1 | convolution fusion | flops 821821440 | bytes 15876097 | tf_op jit(solution)/shard_map/while/body/eval_jaxpr/rkgt,ktd->rkgd/dot_general | solution.py:96
  126.3 4.5 %copy-done.2 = f32[2,1536,256,4]{2,1,3,0:T(8,128)} copy-done((f32[2,1536,256,4]{2,1,3,0:T(8,128)}, f32[2,1536,256,4]{2,1,3,0:T(8,128)S(1)}, u32[]{:S(2)}) %copy-start.2) | copy-done | bytes 12582936 | tf_op jit(solution)/shard_map/while
  133.9 9.7 %fusion.61 = f32[256,2,4,128]{3,0,2,1:T(8,128)} fusion(f32[2,1536,256,4]{2,1,3,0:T(8,128)} %copy-done.2, f32[256,2,4]{0,2,1:T(4,128)S(1)} %select_maximum_fusion.2, pred[256,1536]{0,1:T(8,128)(4,1)S(1)} %concatenate.31, f32[256,2,4,128]{3,0,2,1:T(8,128)} %get-tuple-element.401, bf16[2,2,1536,128]{3,2,1,0:T(8,128)(2,1)S(1)} %copy.35, ...), kind=kOutput, calls=%fused_computation.8.clone.1 | convolution fusion | flops 821821440 | bytes 15876097 | tf_op jit(solution)/shard_map/while/body/eval_jaxpr/rkgt,ktd->rkgd/dot_general | solution.py:96
  151.3 4.5 %copy-done.2 = f32[2,1536,256,4]{2,1,3,0:T(8,128)} copy-done((f32[2,1536,256,4]{2,1,3,0:T(8,128)}, f32[2,1536,256,4]{2,1,3,0:T(8,128)S(1)}, u32[]{:S(2)}) %copy-start.2) | copy-done | bytes 12582936 | tf_op jit(solution)/shard_map/while
  158.9 9.7 %fusion.61 = f32[256,2,4,128]{3,0,2,1:T(8,128)} fusion(f32[2,1536,256,4]{2,1,3,0:T(8,128)} %copy-done.2, f32[256,2,4]{0,2,1:T(4,128)S(1)} %select_maximum_fusion.2, pred[256,1536]{0,1:T(8,128)(4,1)S(1)} %concatenate.31, f32[256,2,4,128]{3,0,2,1:T(8,128)} %get-tuple-element.401, bf16[2,2,1536,128]{3,2,1,0:T(8,128)(2,1)S(1)} %copy.35, ...), kind=kOutput, calls=%fused_computation.8.clone.1 | convolution fusion | flops 821821440 | bytes 15876097 | tf_op jit(solution)/shard_map/while/body/eval_jaxpr/rkgt,ktd->rkgd/dot_general | solution.py:96
  174.7 4.5 %copy-done.2 = f32[2,1536,256,4]{2,1,3,0:T(8,128)} copy-done((f32[2,1536,256,4]{2,1,3,0:T(8,128)}, f32[2,1536,256,4]{2,1,3,0:T(8,128)S(1)}, u32[]{:S(2)}) %copy-start.2) | copy-done | bytes 12582936 | tf_op jit(solution)/shard_map/while
  182.3 9.7 %fusion.61 = f32[256,2,4,128]{3,0,2,1:T(8,128)} fusion(f32[2,1536,256,4]{2,1,3,0:T(8,128)} %copy-done.2, f32[256,2,4]{0,2,1:T(4,128)S(1)} %select_maximum_fusion.2, pred[256,1536]{0,1:T(8,128)(4,1)S(1)} %concatenate.31, f32[256,2,4,128]{3,0,2,1:T(8,128)} %get-tuple-element.401, bf16[2,2,1536,128]{3,2,1,0:T(8,128)(2,1)S(1)} %copy.35, ...), kind=kOutput, calls=%fused_computation.8.clone.1 | convolution fusion | flops 821821440 | bytes 15876097 | tf_op jit(solution)/shard_map/while/body/eval_jaxpr/rkgt,ktd->rkgd/dot_general | solution.py:96
  194.7 7.6 %fusion.21 = (f32[256,2,4]{0,2,1:T(4,128)S(1)}, f32[2,1536,256,4]{2,1,3,0:T(8,128)}) fusion(pred[256,1536]{0,1:T(8,128)(4,1)S(1)} %concatenate.28, bf16[256,2,4,128]{3,0,2,1:T(8,128)(2,1)S(1)} %get-tuple-element.429, bf16[2,2,1536,128]{3,2,1,0:T(8,128)(2,1)} %get-tuple-element.240), kind=kOutput, calls=%fused_computation.28 | convolution fusion | flops 814741504 | bytes 14295040 | tf_op jit(solution)/shard_map/rkgd,ktd->rkgt/dot_general | solution.py:34
  203.8 7.4 %fusion.22 = f32[256,2,4]{0,2,1:T(4,128)S(1)} fusion(f32[2,1536,256,4]{2,1,3,0:T(8,128)} %get-tuple-element.306, f32[256,2,4]{0,2,1:T(4,128)S(1)} %max.13, pred[256,1536]{0,1:T(8,128)(4,1)S(1)} %concatenate.28), kind=kLoop, calls=%fused_computation.29 | loop fusion | flops 15726592 | bytes 12992512 | tf_op jit(solution)/shard_map/reduce_sum | solution.py:95
  212.0 5.0 %divide_convert_fusion = bf16[256,2,4,128]{0,3,2,1:T(8,128)(2,1)S(1)} fusion(f32[2,1536,256,4]{2,1,3,0:T(8,128)S(1)} %copy-done.3, f32[256,2,4]{0,2,1:T(4,128)S(1)} %max.13, pred[256,1536]{0,1:T(8,128)(4,1)S(1)} %concatenate.28, f32[256,2,4,128]{0,3,2,1:T(8,128)} %copy.19, bf16[2,2,1536,128]{2,3,1,0:T(8,128)(2,1)} %copy.20, f32[256,2,4]{0,2,1:T(4,128)S(1)} %bitcast.126, ...), kind=kOutput, calls=%fused_computation.38 | convolution fusion | flops 822083584 | bytes 15360000 | tf_op jit(solution)/shard_map/rkgt,ktd->rkgd/dot_general | solution.py:96
  217.1 3.9 %convolution_convert_fusion = bf16[256,4096]{1,0:T(8,128)(2,1)} fusion(bf16[256,1024]{0,1:T(8,128)(2,1)S(1)} %bitcast.122, bf16[1024,4096]{1,0:T(8,128)(2,1)S(1)} %bitcast.117), kind=kOutput, calls=%fused_computation.33 | convolution fusion | flops 2148532224 | bytes 11010048 | tf_op jit(solution)/shard_map/dot_general | solution.py:120
  220.9 45.5 %reduce-scatter.2.cloned.1.call-done = bf16[256,1024]{1,0:T(8,128)(2,1)} async-done(((bf16[256,4096]{1,0:T(8,128)(2,1)}), bf16[256,1024]{1,0:T(8,128)(2,1)}) %reduce-scatter.2.cloned.1.call-update) | async-done | bytes 524304 | tf_op jit(solution)/shard_map/reduce_scatter | solution.py:121
  (161 shorter events, 75.3 us)
Async XLA Ops:
  6.5 1.6 copy-start
  6.5 259.9 %reduce-scatter.2.cloned.1.call-start = ((), (), s32[]{:S(2)}) async-start(), calls=%async_computation.1 | async-start | bytes 2621440 | tf_op jit(solution)/shard_map/reduce_scatter | solution.py:121
  8.1 8.0 %copy-start.5 = (s32[8]{0:T(128)S(1)}, s32[8]{0:T(128)}, u32[]{:S(2)}) copy-start(s32[8]{0:T(128)} %param.18) | copy-start | bytes 100
  23.6 22.2 %collective-permute-start = (bf16[2,2,1536,128]{3,2,1,0:T(8,128)(2,1)S(1)}, bf16[2,2,1536,128]{3,2,1,0:T(8,128)(2,1)}, u32[]{:S(2)}, u32[]{:S(2)}) collective-permute-start(bf16[2,2,1536,128]{3,2,1,0:T(8,128)(2,1)S(1)} %copy.35), channel_id=1, source_target_pairs={{28,0},{0,4},{4,8},{8,12},{12,16},{16,20},{20,24},{24,28},{29,1},{... | collective-permute-start | bytes 4718600 | tf_op jit(solution)/shard_map/while/body/eval_jaxpr/ppermute | solution.py:16
  28.7 4.5 %copy-start.2 = (f32[2,1536,256,4]{2,1,3,0:T(8,128)}, f32[2,1536,256,4]{2,1,3,0:T(8,128)S(1)}, u32[]{:S(2)}) copy-start(f32[2,1536,256,4]{2,1,3,0:T(8,128)S(1)} %get-tuple-element.379) | copy-start | bytes 37748740 | tf_op jit(solution)/shard_map/while
  47.2 24.6 %collective-permute-start = (bf16[2,2,1536,128]{3,2,1,0:T(8,128)(2,1)S(1)}, bf16[2,2,1536,128]{3,2,1,0:T(8,128)(2,1)}, u32[]{:S(2)}, u32[]{:S(2)}) collective-permute-start(bf16[2,2,1536,128]{3,2,1,0:T(8,128)(2,1)S(1)} %copy.35), channel_id=1, source_target_pairs={{28,0},{0,4},{4,8},{8,12},{12,16},{16,20},{20,24},{24,28},{29,1},{... | collective-permute-start | bytes 4718600 | tf_op jit(solution)/shard_map/while/body/eval_jaxpr/ppermute | solution.py:16
  54.5 4.5 %copy-start.2 = (f32[2,1536,256,4]{2,1,3,0:T(8,128)}, f32[2,1536,256,4]{2,1,3,0:T(8,128)S(1)}, u32[]{:S(2)}) copy-start(f32[2,1536,256,4]{2,1,3,0:T(8,128)S(1)} %get-tuple-element.379) | copy-start | bytes 37748740 | tf_op jit(solution)/shard_map/while
  73.2 22.0 %collective-permute-start = (bf16[2,2,1536,128]{3,2,1,0:T(8,128)(2,1)S(1)}, bf16[2,2,1536,128]{3,2,1,0:T(8,128)(2,1)}, u32[]{:S(2)}, u32[]{:S(2)}) collective-permute-start(bf16[2,2,1536,128]{3,2,1,0:T(8,128)(2,1)S(1)} %copy.35), channel_id=1, source_target_pairs={{28,0},{0,4},{4,8},{8,12},{12,16},{16,20},{20,24},{24,28},{29,1},{... | collective-permute-start | bytes 4718600 | tf_op jit(solution)/shard_map/while/body/eval_jaxpr/ppermute | solution.py:16
  77.9 4.5 %copy-start.2 = (f32[2,1536,256,4]{2,1,3,0:T(8,128)}, f32[2,1536,256,4]{2,1,3,0:T(8,128)S(1)}, u32[]{:S(2)}) copy-start(f32[2,1536,256,4]{2,1,3,0:T(8,128)S(1)} %get-tuple-element.379) | copy-start | bytes 37748740 | tf_op jit(solution)/shard_map/while
  96.6 23.6 %collective-permute-start = (bf16[2,2,1536,128]{3,2,1,0:T(8,128)(2,1)S(1)}, bf16[2,2,1536,128]{3,2,1,0:T(8,128)(2,1)}, u32[]{:S(2)}, u32[]{:S(2)}) collective-permute-start(bf16[2,2,1536,128]{3,2,1,0:T(8,128)(2,1)S(1)} %copy.35), channel_id=1, source_target_pairs={{28,0},{0,4},{4,8},{8,12},{12,16},{16,20},{20,24},{24,28},{29,1},{... | collective-permute-start | bytes 4718600 | tf_op jit(solution)/shard_map/while/body/eval_jaxpr/ppermute | solution.py:16
  102.9 4.5 %copy-start.2 = (f32[2,1536,256,4]{2,1,3,0:T(8,128)}, f32[2,1536,256,4]{2,1,3,0:T(8,128)S(1)}, u32[]{:S(2)}) copy-start(f32[2,1536,256,4]{2,1,3,0:T(8,128)S(1)} %get-tuple-element.379) | copy-start | bytes 37748740 | tf_op jit(solution)/shard_map/while
  121.6 22.0 %collective-permute-start = (bf16[2,2,1536,128]{3,2,1,0:T(8,128)(2,1)S(1)}, bf16[2,2,1536,128]{3,2,1,0:T(8,128)(2,1)}, u32[]{:S(2)}, u32[]{:S(2)}) collective-permute-start(bf16[2,2,1536,128]{3,2,1,0:T(8,128)(2,1)S(1)} %copy.35), channel_id=1, source_target_pairs={{28,0},{0,4},{4,8},{8,12},{12,16},{16,20},{20,24},{24,28},{29,1},{... | collective-permute-start | bytes 4718600 | tf_op jit(solution)/shard_map/while/body/eval_jaxpr/ppermute | solution.py:16
  126.3 4.5 %copy-start.2 = (f32[2,1536,256,4]{2,1,3,0:T(8,128)}, f32[2,1536,256,4]{2,1,3,0:T(8,128)S(1)}, u32[]{:S(2)}) copy-start(f32[2,1536,256,4]{2,1,3,0:T(8,128)S(1)} %get-tuple-element.379) | copy-start | bytes 37748740 | tf_op jit(solution)/shard_map/while
  145.1 23.6 %collective-permute-start = (bf16[2,2,1536,128]{3,2,1,0:T(8,128)(2,1)S(1)}, bf16[2,2,1536,128]{3,2,1,0:T(8,128)(2,1)}, u32[]{:S(2)}, u32[]{:S(2)}) collective-permute-start(bf16[2,2,1536,128]{3,2,1,0:T(8,128)(2,1)S(1)} %copy.35), channel_id=1, source_target_pairs={{28,0},{0,4},{4,8},{8,12},{12,16},{16,20},{20,24},{24,28},{29,1},{... | collective-permute-start | bytes 4718600 | tf_op jit(solution)/shard_map/while/body/eval_jaxpr/ppermute | solution.py:16
  151.3 4.5 %copy-start.2 = (f32[2,1536,256,4]{2,1,3,0:T(8,128)}, f32[2,1536,256,4]{2,1,3,0:T(8,128)S(1)}, u32[]{:S(2)}) copy-start(f32[2,1536,256,4]{2,1,3,0:T(8,128)S(1)} %get-tuple-element.379) | copy-start | bytes 37748740 | tf_op jit(solution)/shard_map/while
  170.1 22.0 %collective-permute-start = (bf16[2,2,1536,128]{3,2,1,0:T(8,128)(2,1)S(1)}, bf16[2,2,1536,128]{3,2,1,0:T(8,128)(2,1)}, u32[]{:S(2)}, u32[]{:S(2)}) collective-permute-start(bf16[2,2,1536,128]{3,2,1,0:T(8,128)(2,1)S(1)} %copy.35), channel_id=1, source_target_pairs={{28,0},{0,4},{4,8},{8,12},{12,16},{16,20},{20,24},{24,28},{29,1},{... | collective-permute-start | bytes 4718600 | tf_op jit(solution)/shard_map/while/body/eval_jaxpr/ppermute | solution.py:16
  174.7 4.5 %copy-start.2 = (f32[2,1536,256,4]{2,1,3,0:T(8,128)}, f32[2,1536,256,4]{2,1,3,0:T(8,128)S(1)}, u32[]{:S(2)}) copy-start(f32[2,1536,256,4]{2,1,3,0:T(8,128)S(1)} %get-tuple-element.379) | copy-start | bytes 37748740 | tf_op jit(solution)/shard_map/while
  192.1 10.3 %copy-start.4 = (f32[256,2,4,128]{3,0,2,1:T(8,128)S(1)}, f32[256,2,4,128]{3,0,2,1:T(8,128)}, u32[]{:S(2)}) copy-start(f32[256,2,4,128]{3,0,2,1:T(8,128)} %get-tuple-element.238) | copy-start | bytes 3145732
  203.8 8.2 %copy-start.3 = (f32[2,1536,256,4]{2,1,3,0:T(8,128)S(1)}, f32[2,1536,256,4]{2,1,3,0:T(8,128)}, u32[]{:S(2)}) copy-start(f32[2,1536,256,4]{2,1,3,0:T(8,128)} %get-tuple-element.306) | copy-start | bytes 37748740
  203.8 13.3 %slice-start = ((s8[8388608]{0:T(1024)(128)(4,1)}), s8[4194304]{0:T(1024)(128)(4,1)S(1)}, s32[]{:S(2)}) async-start(s8[8388608]{0:T(1024)(128)(4,1)} %bitcast.116), calls=%async_computation.2 | async-start | bytes 8388608
  212.0 5.1 %slice-start.1 = ((s8[8388608]{0:T(1024)(128)(4,1)}), s8[4194304]{0:T(1024)(128)(4,1)S(1)}, s32[]{:S(2)}) async-start(s8[8388608]{0:T(1024)(128)(4,1)} %bitcast.116), calls=%async_computation.3 | async-start | bytes 8388608
  212.0 54.5 %copy-start.1 = (bf16[256,4096]{1,0:T(8,128)(2,1)S(1)}, bf16[256,4096]{1,0:T(8,128)(2,1)}, u32[]{:S(2)}) copy-start(bf16[256,4096]{1,0:T(8,128)(2,1)} %param.11) | copy-start | bytes 6291460
Sparse Core Ops, SparseCore 0:
  221.1 45.3 reduce-scatter.1
where the time goes:
time: 274 us; the launch traced here: 273 us
  matrix products  104 us (38%)
  local copies, waits for them, and re-layouts  63.5 us (23%)
  waiting for transfers between devices  45.5 us (17%)
  other arithmetic  39.3 us (14%)
  between operations  13.6 us (5%)
  starting transfers between devices  6.27 us (2%)
    dot_general x8, matrix products, absorb(): jnp.einsum('rkgt,ktd->rkgd', weights.astype(jnp.bfloat16), pair[1], prefe...  73 us
    reduce_scatter x1, waiting for transfers between devices, body(): lax.psum_scatter(partial_out.astype(jnp.bfloat16), 'head', scatter_dimens...  45.5 us
    while x28, local copies, waits for them, and re-layouts  41.4 us
    reduce_sum x8, other arithmetic, absorb(): total = total * factor + jnp.sum(weights, axis=-1)  28.5 us
    dot_general x8, matrix products, block_scores(): jnp.einsum('rkgd,ktd->rkgt', query, keys, preferred_element_type=jnp.floa...  21.8 us
    ppermute x7, starting transfers between devices, shifted(): return lax.ppermute(block, axis, route)  6.27 us
    dot_general x1, matrix products, body(): jnp.dot(join_states, query_weight, preferred_element_type=jnp.float32)  5.71 us
    squeeze x8, local copies, waits for them, and re-layouts, visible_for(): column = lax.dynamic_index_in_dim(visibility, source, 1, keepdims=False)  5.53 us
  transfers between devices with their start and end apart: 8, of which 1 were waited for; matrix products, arithmetic and copies ran while one was open for 45% of the time, Pallas kernels for 0%

commit v1 on v0

v1 whole, which is shorter than its diff:
```python
import functools

import jax
import jax.numpy as jnp
from jax import lax
from jax.experimental import pallas as pl
from jax.experimental.pallas import tpu as pltpu
from jax.sharding import PartitionSpec as P

JSPAN = 32
ROPE_BASE = 500000.0
LOG2E = 1.4426950408889634
HIDE = 1e30
CHUNK = 512
CHAINS = 2
MIB = 1 << 20


def rope_tables(rows, width, first, scale):
    half = width // 2
    freq = ROPE_BASE ** (-(jnp.arange(half, dtype=jnp.float32) * 2.0) / width)
    place = (first + jnp.arange(rows)).astype(jnp.float32)
    angle = place[:, None] * freq[None, :]
    cosine = jnp.cos(angle) * scale
    sine = jnp.sin(angle) * scale
    return jnp.concatenate([cosine, cosine], axis=1), jnp.concatenate([-sine, sine], axis=1)


def attend_kernel(per_kv, blocks_each, at_ref, lengths_ref, seen_ref, q_ref, ok_ref, ov_ref, bk_ref, bv_ref,
                  o_ref, stat_ref, ov_wide, bv_wide, order):
    width = ok_ref.shape[2]
    me = at_ref[1]
    length = lengths_ref[me]
    blocks = q_ref.shape[0] // JSPAN
    branch_most = bk_ref.shape[1]
    chunk = min(CHUNK, branch_most)
    ov_wide[:, :width] = ov_ref[0]
    ov_wide[:, width:] = jnp.ones((ov_ref.shape[1], width), jnp.bfloat16)
    bv_wide[:, :width] = bv_ref[0]
    bv_wide[:, width:] = jnp.ones((branch_most, width), jnp.bfloat16)

    def place(block, ends):
        front, back = ends
        hit = seen_ref[block, me] == 1
        order[jnp.where(hit, front, back)] = block
        step = hit.astype(jnp.int32)
        return front + step, back - 1 + step

    seen_count, _ = lax.fori_loop(0, blocks, place, (jnp.int32(0), jnp.int32(blocks - 1)))

    def scores(query, keys):
        return lax.dot_general(query, keys, (((1,), (1,)), ((), ())), preferred_element_type=jnp.float32)

    tile = blocks_each * JSPAN
    per_turn = CHAINS * blocks_each

    def turn(step, _):
        base = step * per_turn
        starts, queries, states, shown = [], [], [], []
        row = lax.broadcasted_iota(jnp.int32, (per_kv * tile, 1), 0)
        slot = (row // JSPAN) % blocks_each
        for chain in range(CHAINS):
            first = base + chain * blocks_each
            at = [pl.multiple_of(order[first + j] * JSPAN, JSPAN) for j in range(blocks_each)]
            starts.append(at)
            queries.append(jnp.concatenate(
                [q_ref[pl.ds(at[j], JSPAN), h * width:(h + 1) * width] for h in range(per_kv) for j in range(blocks_each)],
                axis=0))
            shown.append(first + slot < seen_count)
        for chain in range(CHAINS):
            s = scores(queries[chain], ok_ref[0])
            best = jnp.max(s, axis=1, keepdims=True)
            weights = jnp.exp2(s - best).astype(jnp.bfloat16)
            states += [best, jnp.dot(weights, ov_wide[...], preferred_element_type=jnp.float32)]

        def more(part, state):
            begin = pl.multiple_of(part * chunk, chunk)
            keys = bk_ref[0, pl.ds(begin, chunk), :]
            values = bv_wide[pl.ds(begin, chunk), :]
            place_in = begin + lax.broadcasted_iota(jnp.int32, (1, chunk), 1)
            bias = jnp.where(place_in < length, 0.0, -HIDE)
            out = []
            for chain in range(CHAINS):
                best, acc = state[2 * chain], state[2 * chain + 1]
                s = scores(queries[chain], keys) + bias
                grown = jnp.maximum(best, jnp.max(s, axis=1, keepdims=True))
                new_best = jnp.where(shown[chain], grown, best)
                weights = jnp.exp2(s - jnp.where(shown[chain], grown, HIDE)).astype(jnp.bfloat16)
                acc = acc * jnp.exp2(best - new_best) + jnp.dot(weights, values, preferred_element_type=jnp.float32)
                out += [new_best, acc]
            return tuple(out)

        parts = jnp.where(base < seen_count, (length + chunk - 1) // chunk, 0)
        states = lax.fori_loop(0, parts, more, tuple(states))
        for chain in range(CHAINS):
            best, acc = states[2 * chain], states[2 * chain + 1]
            total = acc[:, width:]
            part_out = (acc[:, :width] / total).astype(o_ref.dtype)
            logs = best + jnp.log2(total[:, :1])
            for h in range(per_kv):
                for j in range(blocks_each):
                    here = (h * blocks_each + j) * JSPAN
                    rows = pl.ds(starts[chain][j], JSPAN)
                    o_ref[rows, h * width:(h + 1) * width] = part_out[here:here + JSPAN]
                    stat_ref[rows, h:h + 1] = logs[here:here + JSPAN]
        return 0

    lax.fori_loop(0, blocks // per_turn, turn, 0)


def attend(query, kv, me, lengths, seen, outline_keys, outline_values, branch_keys, branch_values):
    rows, columns = query.shape
    width = outline_keys.shape[2]
    per_kv = columns // width
    outline_here, branch_most = outline_keys.shape[1], branch_keys.shape[1]
    whole = lambda i, at, lens, vis: (0, 0)
    one = lambda i, at, lens, vis: (at[0], 0, 0)
    keys_all = outline_here + branch_most // 2
    return pl.pallas_call(
        functools.partial(attend_kernel, per_kv, 2),
        out_shape=(jax.ShapeDtypeStruct((rows, columns), jnp.bfloat16), jax.ShapeDtypeStruct((rows, per_kv), jnp.float32)),
        grid_spec=pltpu.PrefetchScalarGridSpec(
            num_scalar_prefetch=3,
            grid=(1,),
            in_specs=[
                pl.BlockSpec((rows, columns), whole),
                pl.BlockSpec((1, outline_here, width), one),
                pl.BlockSpec((1, outline_here, width), one),
                pl.BlockSpec((1, branch_most, width), one),
                pl.BlockSpec((1, branch_most, width), one),
            ],
            out_specs=(pl.BlockSpec((rows, columns), whole), pl.BlockSpec((rows, per_kv), whole)),
            scratch_shapes=[
                pltpu.VMEM((outline_here, 2 * width), jnp.bfloat16),
                pltpu.VMEM((branch_most, 2 * width), jnp.bfloat16),
                pltpu.SMEM((rows // JSPAN,), jnp.int32),
            ],
        ),
        compiler_params=pltpu.CompilerParams(vmem_limit_bytes=40 * MIB),
        cost_estimate=pl.CostEstimate(
            flops=rows * columns * keys_all * 8, bytes_accessed=4 * rows * columns, transcendentals=rows * per_kv * keys_all),
        name="attend",
    )(jnp.stack([kv, me]).astype(jnp.int32), lengths, seen, query, outline_keys, outline_values, branch_keys, branch_values)


def body(join_states, query_weight, out_weight, outline_keys, outline_values, branch_keys, branch_values, branch_lengths, visibility):
    width = outline_keys.shape[2]
    head_count = query_weight.shape[1] // width
    group = head_count * lax.axis_size("head") // outline_keys.shape[0]
    kv_local = max(1, head_count // group)
    per_kv = head_count // kv_local
    kv_start = lax.axis_index("head") * head_count // group
    rows = join_states.shape[0]
    n_ctx = lax.axis_size("ctx")
    me = lax.axis_index("ctx")
    first = outline_keys.shape[1] * n_ctx + branch_keys.shape[1] + me * rows
    cosine, sine = rope_tables(rows, width, first, width ** (-0.5) * LOG2E)
    columns = per_kv * width
    gathered = []
    for kv in range(kv_local):
        queries = jnp.dot(join_states, query_weight[:, kv * columns:(kv + 1) * columns], preferred_element_type=jnp.float32)
        queries = queries.reshape(rows, per_kv, width)
        turned = jnp.concatenate([queries[..., width // 2:], queries[..., :width // 2]], axis=-1)
        rotated = (queries * cosine[:, None, :] + turned * sine[:, None, :]).astype(jnp.bfloat16)
        gathered.append(lax.all_gather(rotated.reshape(rows, columns), "ctx", axis=0, tiled=True))
    parts, logs = [], []
    for kv in range(kv_local):
        part, log = attend(gathered[kv], kv_start + kv, me, branch_lengths, visibility,
                           outline_keys, outline_values, branch_keys, branch_values)
        parts.append(lax.all_to_all(part, "ctx", 0, 0, tiled=True).reshape(n_ctx, rows, per_kv, width))
        logs.append(log)
    logs = lax.all_to_all(jnp.concatenate(logs, axis=1), "ctx", 0, 0, tiled=True).reshape(n_ctx, rows, kv_local, per_kv)
    share = jnp.exp2(logs - jnp.max(logs, axis=0, keepdims=True))
    share = share / jnp.sum(share, axis=0, keepdims=True)
    mixed = [jnp.sum(share[:, :, kv, :, None] * parts[kv].astype(jnp.float32), axis=0).astype(jnp.bfloat16).reshape(rows, columns)
             for kv in range(kv_local)]
    mixed = jnp.concatenate(mixed, axis=1)
    partial_out = jnp.dot(mixed, out_weight, preferred_element_type=jnp.float32)
    return lax.psum_scatter(partial_out.astype(jnp.bfloat16), "head", scatter_dimension=1, tiled=True)


def solution(mesh):
    return jax.shard_map(
        body,
        mesh=mesh,
        in_specs=(P("ctx", None), P(None, "head"), P("head", None), P(None, "ctx", None), P(None, "ctx", None),
                  P(None, "ctx", None), P(None, "ctx", None), P(), P()),
        out_specs=P("ctx", "head"),
        check_vma=False,
    )
```

time: 274 us -> 254 us (0.927); the launches traced: 273 us -> 257 us
  matrix products: 104 us -> 12.1 us
  Pallas kernels: 0 us -> 62.8 us
  blocking collectives: 0 us -> 40.6 us
  waiting for transfers between devices: 45.5 us -> 76.7 us
  other arithmetic: 39.3 us -> 9.06 us
  local copies, waits for them, and re-layouts: 63.5 us -> 38.5 us
    dot_general x17 -> x2, matrix products: 101 us -> 4.88 us  [body(): jnp.dot(join_states, query_weight[:, kv * columns:(kv + 1) * columns], pr...]
    pallas_call x0 -> x2, Pallas kernels: none -> 62.8 us  [attend(): pl.pallas_call(functools.partial(attend_kernel, per_kv, 2), out_shape=(ja...]
    while x30 -> x0, local copies, waits for them, and re-layouts: 45.5 us -> none
    all_to_all x0 -> x2, blocking collectives: none -> 40.6 us  [the longest x1 29.8 us: body(): lax.all_to_all(part, 'ctx', 0, 0, tiled=True)]
    all_gather x0 -> x2, waiting for transfers between devices: none -> 29.7 us  [body(): lax.all_gather(rotated.reshape(rows, columns), 'ctx', axis=0, tiled=True)]
    reduce_sum x8 -> x3, other arithmetic: 28.5 us -> 6.43 us  [the longest x2 6.41 us: body(): jnp.sum(share[:, :, kv, :, None] * parts[kv].astype(jnp.float32), axis=0)]
    mul x0 -> x8, local copies, waits for them, and re-layouts: none -> 19.6 us  [the longest x7 19.5 us: body(): share[:, :, kv, :, None] * parts[kv].astype(jnp.float32)]
    unnamed x15 -> x31, local copies, waits for them, and re-layouts: 2.53 us -> 17.2 us
  transfers between devices with their start and end apart: 8 -> 4, of which waited for: 1 -> 3; matrix products, arithmetic and copies ran while one was open for 45% -> 9% of each run, Pallas kernels for 0% -> 12%
where the time goes in v1:
time: 254 us; the launch traced here: 257 us
  waiting for transfers between devices  76.7 us (30%)
  Pallas kernels  62.8 us (25%)
  blocking collectives  40.6 us (16%)
  local copies, waits for them, and re-layouts  38.5 us (15%)
  between operations  13.3 us (5%)
  matrix products  12.1 us (5%)
  other arithmetic  9.06 us (4%)
  starting transfers between devices  3.87 us (2%)
    pallas_call x2, Pallas kernels, attend(): pl.pallas_call(functools.partial(attend_kernel, per_kv, 2), out_shape=(ja...  62.8 us
    reduce_scatter x1, waiting for transfers between devices, body(): lax.psum_scatter(partial_out.astype(jnp.bfloat16), 'head', scatter_dimens...  43.1 us
    all_to_all x1, blocking collectives, body(): lax.all_to_all(part, 'ctx', 0, 0, tiled=True)  29.8 us
    all_gather x2, waiting for transfers between devices, body(): lax.all_gather(rotated.reshape(rows, columns), 'ctx', axis=0, tiled=True)  29.7 us
    mul x7, local copies, waits for them, and re-layouts, body(): share[:, :, kv, :, None] * parts[kv].astype(jnp.float32)  19.5 us
    unnamed x31, local copies, waits for them, and re-layouts  17.2 us
    all_to_all x1, blocking collectives, body(): lax.all_to_all(jnp.concatenate(logs, axis=1), 'ctx', 0, 0, tiled=True)  10.9 us
    dot_general x1, matrix products, body(): partial_out = jnp.dot(mixed, out_weight, preferred_element_type=jnp.float32)  7.21 us
  transfers between devices with their start and end apart: 4, of which 3 were waited for; matrix products, arithmetic and copies ran while one was open for 9% of the time, Pallas kernels for 12%

profile of v1, /device:TPU:0, one launch (start us, length us, event | category | flops | bytes accessed | tf_op | source)
XLA Modules:
  0.0 257.0 jit_solution(7015229666411275411)
XLA Ops:
  6.6 1.6 copy-done
  8.1 3.6 %fusion.2 = f32[256,512]{1,0:T(8,128)S(1)} fusion(bf16[256,4096]{1,0:T(8,128)(2,1)S(1)} %copy-done, bf16[4096,1024]{1,0:T(8,128)(2,1)} %param.10), kind=kOutput, calls=%fused_computation.5 | convolution fusion | flops 1073741824 | bytes 6815744 | tf_op jit(solution)/shard_map/dot_general | solution.py:161
  12.8 1.3 fusion
  18.7 29.7 %all-gather.3.cloned.1.call-done.q_ref = bf16[2048,512]{1,0:T(8,128)(2,1)} async-done(((bf16[256,512]{1,0:T(8,128)(2,1)}), bf16[2048,512]{1,0:T(8,128)(2,1)}) %all-gather.3.cloned.1.call-update) | async-done | bytes 2097168 | tf_op jit(solution)/shard_map/all_gather | solution.py:165
  48.4 1.6 copy-done.2
  50.0 1.6 copy-done.4
  51.6 1.6 copy-done.6
  55.6 30.7 %attend.2 = (bf16[2048,512]{1,0:T(8,128)(2,1)S(1)}, f32[2048,4]{1,0:T(8,128)S(1)}) custom-call(s32[2]{0:T(128)S(1)} %pad_add_fusion.at_ref, s32[8]{0:T(128)S(1)} %copy-done.12, s32[64,8]{1,0:T(8,128)S(1)} %copy.17.seen_ref, bf16[2048,512]{1,0:T(8,128)(2,1)S(1)} %copy-done.6, bf16[8,512,128]{2,1,0:T(8,128)(2,1)S(1)} %copy-done.8, ...), custom_call_target="tpu_custom_call" | custom-call | flops 8589934592 | bytes 4194304 | tf_op jit(solution)/shard_map/attend/pallas_call | solution.py:119
  86.7 1.6 copy-done.3
  88.3 1.6 copy-done.5
  89.9 1.6 copy-done.7
  94.0 32.0 %attend.3 = (bf16[2048,512]{1,0:T(8,128)(2,1)}, f32[2048,4]{1,0:T(8,128)S(1)}) custom-call(s32[2]{0:T(128)S(1)} %pad_add_fusion.1.at_ref, s32[8]{0:T(128)S(1)} %copy-done.12, s32[64,8]{1,0:T(8,128)S(1)} %copy.17.seen_ref, bf16[2048,512]{1,0:T(8,128)(2,1)S(1)} %copy-done.7, bf16[8,512,128]{2,1,0:T(8,128)(2,1)S(1)} %copy-done.9, ...), custom_call_target="tpu_custom_call" | custom-call | flops 8589934592 | bytes 4194304 | tf_op jit(solution)/shard_map/attend/pallas_call | solution.py:119
  126.4 10.9 %all_to_all.27 = f32[8,256,8]{1,2,0:T(8,128)S(1)} all-to-all(f32[8,256,8]{1,2,0:T(8,128)S(1)} %bitcast.41), channel_id=1, replica_groups=mesh['ctx'=8,'head'=4] {'ctx'}, dimensions={0} | all-to-all | bytes 131072 | tf_op jit(solution)/shard_map/all_to_all | solution.py:172
  137.2 29.8 %all_to_all.28 = bf16[8,256,512]{2,1,0:T(8,128)(2,1)} all-to-all(bf16[8,256,512]{2,1,0:T(8,128)(2,1)S(1)} %bitcast.36), channel_id=1, replica_groups=mesh['ctx'=8,'head'=4] {'ctx'}, dimensions={0} | all-to-all | bytes 4194304 | tf_op jit(solution)/shard_map/all_to_all | solution.py:170
  167.0 3.6 %all-to-all-start.2 = ((bf16[8,256,512]{2,1,0:T(8,128)(2,1)}), bf16[8,256,512]{2,1,0:T(8,128)(2,1)S(1)}, u32[]{:S(2)}, u32[]{:S(2)}) async-start(bf16[8,256,512]{2,1,0:T(8,128)(2,1)} %bitcast.8), calls=%async_computation.2 | async-start | bytes 4194304 | tf_op jit(solution)/shard_map/all_to_all | solution.py:170
  171.4 3.9 %mul.120 = f32[8,256,4,128]{3,2,1,0:T(4,128)} broadcast(f32[8,256,4]{2,1,0:T(8,128)S(1)} %copy.22), dimensions={0,1,2} | broadcast | bytes 4227072 | tf_op jit(solution)/shard_map/mul | solution.py:175
  175.2 5.5 %mul.121 = f32[8,256,512]{2,1,0:T(8,128)} reshape(f32[8,256,4,128]{3,2,1,0:T(4,128)} %mul.120) | data formatting | bytes 8388608 | tf_op jit(solution)/shard_map/mul | solution.py:175
  181.1 3.9 %mul.124 = f32[8,256,4,128]{3,2,1,0:T(4,128)} broadcast(f32[8,256,4]{2,1,0:T(8,128)S(1)} %copy.23), dimensions={0,1,2} | broadcast | bytes 4227072 | tf_op jit(solution)/shard_map/mul | solution.py:175
  185.0 5.5 %mul.125 = f32[8,256,512]{2,1,0:T(8,128)} reshape(f32[8,256,4,128]{3,2,1,0:T(4,128)} %mul.124) | data formatting | bytes 8388608 | tf_op jit(solution)/shard_map/mul | solution.py:175
  190.5 3.5 %multiply_reduce_fusion.1 = bf16[256,512]{1,0:T(8,128)(2,1)S(1)} fusion(f32[8,256,512]{2,1,0:T(8,128)} %mul.121, bf16[8,256,512]{2,1,0:T(8,128)(2,1)} %all_to_all.28), kind=kLoop, calls=%fused_computation.2 | loop fusion | flops 3014656 | bytes 6553600 | tf_op jit(solution)/shard_map/reduce_sum | solution.py:175
  194.1 3.1 %all-to-all-done.2 = bf16[8,256,512]{2,1,0:T(8,128)(2,1)S(1)} async-done(((bf16[8,256,512]{2,1,0:T(8,128)(2,1)}), bf16[8,256,512]{2,1,0:T(8,128)(2,1)S(1)}, u32[]{:S(2)}, u32[]{:S(2)}) %all-to-all-start.2) | async-done | bytes 2097184 | tf_op jit(solution)/shard_map/all_to_all | solution.py:170
  197.2 2.9 %multiply_reduce_fusion = bf16[256,512]{1,0:T(8,128)(2,1)S(1)} fusion(f32[8,256,512]{2,1,0:T(8,128)} %mul.125, bf16[8,256,512]{2,1,0:T(8,128)(2,1)S(1)} %all-to-all-done.2), kind=kLoop, calls=%fused_computation.1 | loop fusion | flops 3014656 | bytes 6553600 | tf_op jit(solution)/shard_map/reduce_sum | solution.py:175
  200.1 7.2 %convolution_convert_fusion = bf16[256,4096]{1,0:T(8,128)(2,1)} fusion(bf16[1024,4096]{1,0:T(8,128)(2,1)} %param.11, bf16[256,512]{1,0:T(8,128)(2,1)S(1)} %multiply_reduce_fusion, bf16[256,512]{1,0:T(8,128)(2,1)S(1)} %multiply_reduce_fusion.1), kind=kOutput, calls=%fused_computation | convolution fusion | flops 2149580800 | bytes 11010048 | tf_op jit(solution)/shard_map/dot_general | solution.py:178
  207.3 43.1 %reduce-scatter.2.cloned.1.call-done = bf16[256,1024]{1,0:T(8,128)(2,1)} async-done(((bf16[256,4096]{1,0:T(8,128)(2,1)}), bf16[256,1024]{1,0:T(8,128)(2,1)}) %reduce-scatter.2.cloned.1.call-update) | async-done | bytes 524304 | tf_op jit(solution)/shard_map/reduce_scatter | solution.py:179
  (55 shorter events, 12.2 us)
Async XLA Ops:
  6.5 1.6 copy-start
  6.5 41.9 %all-gather.3.cloned.1.call-start = ((), (), s32[]{:S(2)}) async-start(), calls=%async_computation.4 | async-start | bytes 2359296 | tf_op jit(solution)/shard_map/all_gather | solution.py:165
  8.1 4.6 %copy-start.14 = (bf16[4096,1024]{1,0:T(8,128)(2,1)S(1)}, bf16[4096,1024]{1,0:T(8,128)(2,1)}, u32[]{:S(2)}) copy-start(bf16[4096,1024]{1,0:T(8,128)(2,1)} %param.10) | copy-start | bytes 25165828
  15.6 2.8 %copy-start.13 = (s32[64,8]{0,1:T(8,128)S(1)}, s32[64,8]{0,1:T(8,128)}, u32[]{:S(2)}) copy-start(s32[64,8]{0,1:T(8,128)} %param.17) | copy-start | bytes 6148
  15.7 32.8 %copy-start.12 = (s32[8]{0:T(128)S(1)}, s32[8]{0:T(128)}, u32[]{:S(2)}) copy-start(s32[8]{0:T(128)} %lengths_ref.3) | copy-start | bytes 100
  17.7 69.1 %all-gather.5.cloned.1.call-start = ((), (), s32[]{:S(2)}) async-start(), calls=%async_computation.5 | async-start | bytes 2359296 | tf_op jit(solution)/shard_map/all_gather | solution.py:165
  48.4 1.6 copy-start.2
  50.0 1.6 copy-start.4
  51.6 1.6 copy-start.6
  53.2 1.2 copy-start.8
  54.4 1.2 copy-start.10
  86.7 1.6 copy-start.3
  88.3 1.6 copy-start.5
  89.9 1.6 copy-start.7
  91.5 1.2 copy-start.9
  92.7 1.2 copy-start.11
  167.0 30.2 %all-to-all-start.2 = ((bf16[8,256,512]{2,1,0:T(8,128)(2,1)}), bf16[8,256,512]{2,1,0:T(8,128)(2,1)S(1)}, u32[]{:S(2)}, u32[]{:S(2)}) async-start(bf16[8,256,512]{2,1,0:T(8,128)(2,1)} %bitcast.8), calls=%async_computation.2 | async-start | bytes 4194304 | tf_op jit(solution)/shard_map/all_to_all | solution.py:170
  170.6 79.8 %reduce-scatter.2.cloned.1.call-start = ((), (), s32[]{:S(2)}) async-start(), calls=%async_computation.6 | async-start | bytes 2621440 | tf_op jit(solution)/shard_map/reduce_scatter | solution.py:179
  200.0 50.4 %copy-start.1 = (bf16[256,4096]{1,0:T(8,128)(2,1)S(1)}, bf16[256,4096]{1,0:T(8,128)(2,1)}, u32[]{:S(2)}) copy-start(bf16[256,4096]{1,0:T(8,128)(2,1)} %param.9) | copy-start | bytes 6291460
Sparse Core Ops, SparseCore 0:
  17.8 30.5 all-gather.2
  50.3 27.8 all-gather.4
  207.4 42.9 reduce-scatter.1

commit v2 on v1

--- a/solution.py
+++ b/solution.py
@@ -13,6 +13,7 @@
 HIDE = 1e30
 CHUNK = 512
 CHAINS = 2
+PAD = 16
 MIB = 1 << 20
 
 
@@ -27,17 +28,18 @@
 
 
 def attend_kernel(per_kv, blocks_each, at_ref, lengths_ref, seen_ref, q_ref, ok_ref, ov_ref, bk_ref, bv_ref,
-                  o_ref, stat_ref, ov_wide, bv_wide, order):
+                  o_ref, stat_ref, ov_turned, bv_turned, order):
     width = ok_ref.shape[2]
     me = at_ref[1]
     length = lengths_ref[me]
     blocks = q_ref.shape[0] // JSPAN
     branch_most = bk_ref.shape[1]
     chunk = min(CHUNK, branch_most)
-    ov_wide[:, :width] = ov_ref[0]
-    ov_wide[:, width:] = jnp.ones((ov_ref.shape[1], width), jnp.bfloat16)
-    bv_wide[:, :width] = bv_ref[0]
-    bv_wide[:, width:] = jnp.ones((branch_most, width), jnp.bfloat16)
+    ov_turned[:width, :] = ov_ref[0].T
+    ov_turned[width:, :] = jnp.ones((PAD, ov_ref.shape[1]), jnp.bfloat16)
+    for part in range(branch_most // chunk):
+        bv_turned[part, :width, :] = bv_ref[0, part * chunk:(part + 1) * chunk].T
+        bv_turned[part, width:, :] = jnp.ones((PAD, chunk), jnp.bfloat16)
 
     def place(block, ends):
         front, back = ends
@@ -48,8 +50,8 @@
 
     seen_count, _ = lax.fori_loop(0, blocks, place, (jnp.int32(0), jnp.int32(blocks - 1)))
 
-    def scores(query, keys):
-        return lax.dot_general(query, keys, (((1,), (1,)), ((), ())), preferred_element_type=jnp.float32)
+    def scores(keys, query):
+        return lax.dot_general(keys, query, (((1,), (1,)), ((), ())), preferred_element_type=jnp.float32)
 
     tile = blocks_each * JSPAN
     per_turn = CHAINS * blocks_each
@@ -57,8 +59,8 @@
     def turn(step, _):
         base = step * per_turn
         starts, queries, states, shown = [], [], [], []
-        row = lax.broadcasted_iota(jnp.int32, (per_kv * tile, 1), 0)
-        slot = (row // JSPAN) % blocks_each
+        column = lax.broadcasted_iota(jnp.int32, (1, per_kv * tile), 1)
+        slot = (column // JSPAN) % blocks_each
         for chain in range(CHAINS):
             first = base + chain * blocks_each
             at = [pl.multiple_of(order[first + j] * JSPAN, JSPAN) for j in range(blocks_each)]
@@ -68,25 +70,25 @@
                 axis=0))
             shown.append(first + slot < seen_count)
         for chain in range(CHAINS):
-            s = scores(queries[chain], ok_ref[0])
-            best = jnp.max(s, axis=1, keepdims=True)
+            s = scores(ok_ref[0], queries[chain])
+            best = jnp.max(s, axis=0, keepdims=True)
             weights = jnp.exp2(s - best).astype(jnp.bfloat16)
-            states += [best, jnp.dot(weights, ov_wide[...], preferred_element_type=jnp.float32)]
+            states += [best, jnp.dot(ov_turned[...], weights, preferred_element_type=jnp.float32)]
 
         def more(part, state):
             begin = pl.multiple_of(part * chunk, chunk)
             keys = bk_ref[0, pl.ds(begin, chunk), :]
-            values = bv_wide[pl.ds(begin, chunk), :]
-            place_in = begin + lax.broadcasted_iota(jnp.int32, (1, chunk), 1)
+            values = bv_turned[part]
+            place_in = begin + lax.broadcasted_iota(jnp.int32, (chunk, 1), 0)
             bias = jnp.where(place_in < length, 0.0, -HIDE)
             out = []
             for chain in range(CHAINS):
                 best, acc = state[2 * chain], state[2 * chain + 1]
-                s = scores(queries[chain], keys) + bias
-                grown = jnp.maximum(best, jnp.max(s, axis=1, keepdims=True))
+                s = scores(keys, queries[chain]) + bias
+                grown = jnp.maximum(best, jnp.max(s, axis=0, keepdims=True))
                 new_best = jnp.where(shown[chain], grown, best)
                 weights = jnp.exp2(s - jnp.where(shown[chain], grown, HIDE)).astype(jnp.bfloat16)
-                acc = acc * jnp.exp2(best - new_best) + jnp.dot(weights, values, preferred_element_type=jnp.float32)
+                acc = acc * jnp.exp2(best - new_best) + jnp.dot(values, weights, preferred_element_type=jnp.float32)
                 out += [new_best, acc]
             return tuple(out)
 
@@ -94,15 +96,15 @@
         states = lax.fori_loop(0, parts, more, tuple(states))
         for chain in range(CHAINS):
             best, acc = states[2 * chain], states[2 * chain + 1]
-            total = acc[:, width:]
-            part_out = (acc[:, :width] / total).astype(o_ref.dtype)
-            logs = best + jnp.log2(total[:, :1])
+            total = acc[width:width + 8]
+            part_out = (acc[:width] * (1.0 / total[:1])).T.astype(o_ref.dtype)
+            logs = jnp.concatenate([best + jnp.log2(total), jnp.zeros((width - 8, per_kv * tile), jnp.float32)], axis=0).T
             for h in range(per_kv):
                 for j in range(blocks_each):
                     here = (h * blocks_each + j) * JSPAN
                     rows = pl.ds(starts[chain][j], JSPAN)
                     o_ref[rows, h * width:(h + 1) * width] = part_out[here:here + JSPAN]
-                    stat_ref[rows, h:h + 1] = logs[here:here + JSPAN]
+                    stat_ref[rows, h:h + 1] = logs[here:here + JSPAN, :1]
         return 0
 
     lax.fori_loop(0, blocks // per_turn, turn, 0)
@@ -131,16 +133,129 @@
             ],
             out_specs=(pl.BlockSpec((rows, columns), whole), pl.BlockSpec((rows, per_kv), whole)),
             scratch_shapes=[
-                pltpu.VMEM((outline_here, 2 * width), jnp.bfloat16),
-                pltpu.VMEM((branch_most, 2 * width), jnp.bfloat16),
+                pltpu.VMEM((width + PAD, outline_here), jnp.bfloat16),
+                pltpu.VMEM((branch_most // min(CHUNK, branch_most), width + PAD, min(CHUNK, branch_most)), jnp.bfloat16),
                 pltpu.SMEM((rows // JSPAN,), jnp.int32),
             ],
         ),
-        compiler_params=pltpu.CompilerParams(vmem_limit_bytes=40 * MIB),
+        compiler_params=pltpu.CompilerParams(vmem_limit_bytes=60 * MIB),
         cost_estimate=pl.CostEstimate(
             flops=rows * columns * keys_all * 8, bytes_accessed=4 * rows * columns, transcendentals=rows * per_kv * keys_all),
         name="attend",
     )(jnp.stack([kv, me]).astype(jnp.int32), lengths, seen, query, outline_keys, outline_values, branch_keys, branch_values)
+
+
+def return_kernel(n_ctx, kv_local, heads, *refs):
+    parts = refs[:kv_local]
+    logs_ref, mixed_ref, near, near_logs, joined, joined_logs, far, far_logs = refs[kv_local:kv_local + 8]
+    near_sems, far_sems = refs[kv_local + 8:]
+    rows, columns = near.shape[2:]
+    width = kv_local * columns // heads
+    per_kv = columns // width
+    chips = n_ctx // 2
+    me = lax.axis_index("ctx")
+    chip, core = me // 2, me % 2
+    sibling = chip * 2 + 1 - core
+
+    def peer(j):
+        return ((chip + j) % chips) * 2
+
+    def copy(src, dst, sems, which, device):
+        return pltpu.make_async_remote_copy(
+            src_ref=src, dst_ref=dst, send_sem=sems.at[0, which], recv_sem=sems.at[1, which],
+            device_id={"ctx": device}, device_id_type=pl.DeviceIdType.MESH)
+
+    barrier = pltpu.get_barrier_semaphore()
+    pl.semaphore_signal(barrier, inc=1, device_id={"ctx": sibling}, device_id_type=pl.DeviceIdType.MESH)
+    for j in range(1, chips):
+        pl.semaphore_signal(barrier, inc=1, device_id={"ctx": peer(j) + core}, device_id_type=pl.DeviceIdType.MESH)
+    pl.semaphore_wait(barrier, chips)
+
+    def spread(shares):
+        filled = jnp.concatenate([shares, jnp.zeros((128 - shares.shape[0], rows), jnp.float32)], axis=0)
+        return filled.T
+
+    sequence = [(j + 1) % chips for j in range(chips)]
+    sequence = sequence[::-1][1:] + [0] if chips > 1 else sequence
+    near_copies = {}
+    for j in sequence:
+        block = peer(j) + 1 - core
+        mine = pl.ds(pl.multiple_of(block * rows, rows), rows)
+        group = [copy(logs_ref.at[block], near_logs.at[j], near_sems, j * (kv_local + 1) + kv_local, sibling)]
+        for kv in range(kv_local):
+            group.append(copy(parts[kv].at[mine], near.at[j, kv], near_sems, j * (kv_local + 1) + kv, sibling))
+        for c in group:
+            c.start()
+        near_copies[j] = group
+    far_copies = {}
+    for j in sequence:
+        for c in near_copies[j]:
+            c.wait_recv()
+        block = peer(j) + core
+        own, other = logs_ref[block], near_logs[j]
+        top = jnp.maximum(own, other)
+        own_share, other_share = jnp.exp2(own - top), jnp.exp2(other - top)
+        total = own_share + other_share
+        joined_logs[j] = top + jnp.log2(total)
+        own_wide, other_wide = spread(own_share / total), spread(other_share / total)
+        mine = pl.ds(pl.multiple_of(block * rows, rows), rows)
+        for kv in range(kv_local):
+            for h in range(per_kv):
+                at, head = slice(h * width, (h + 1) * width), kv * per_kv + h
+                value = (parts[kv][mine, at].astype(jnp.float32) * own_wide[:, head:head + 1]
+                         + near[j, kv, :, at].astype(jnp.float32) * other_wide[:, head:head + 1])
+                joined[j, kv, :, at] = value.astype(jnp.bfloat16)
+        if j > 0:
+            group = [copy(joined_logs.at[j], far_logs.at[j - 1], far_sems, 2 * (j - 1) + 1, peer(j) + core),
+                     copy(joined.at[j], far.at[j - 1], far_sems, 2 * (j - 1), peer(j) + core)]
+            for c in group:
+                c.start()
+            far_copies[j] = group
+    for j in range(1, chips):
+        for c in far_copies[j]:
+            c.wait_recv()
+    every = [joined_logs[0]] + [far_logs[j] for j in range(chips - 1)]
+    top = functools.reduce(jnp.maximum, every)
+    shares = [jnp.exp2(x - top) for x in every]
+    total = functools.reduce(jnp.add, shares)
+    wide = [spread(x / total) for x in shares]
+    for kv in range(kv_local):
+        for h in range(per_kv):
+            at, head = slice(h * width, (h + 1) * width), kv * per_kv + h
+            value = joined[0, kv, :, at].astype(jnp.float32) * wide[0][:, head:head + 1]
+            for j in range(chips - 1):
+                value += far[j, kv, :, at].astype(jnp.float32) * wide[j + 1][:, head:head + 1]
+            mixed_ref[:, head * width:(head + 1) * width] = value.astype(jnp.bfloat16)
+    for j in sequence:
+        for c in near_copies[j] + far_copies.get(j, []):
+            c.wait_send()
+
+
+def give_back(parts, logs, n_ctx, heads):
+    kv_local = len(parts)
+    rows, columns = parts[0].shape[0] // n_ctx, parts[0].shape[1]
+    chips = n_ctx // 2
+    fars = max(chips - 1, 1)
+    tall = logs.shape[1]
+    vmem = pl.BlockSpec(memory_space=pltpu.VMEM)
+    return pl.pallas_call(
+        functools.partial(return_kernel, n_ctx, kv_local, heads),
+        out_shape=jax.ShapeDtypeStruct((rows, kv_local * columns), jnp.bfloat16),
+        in_specs=[vmem] * (kv_local + 1),
+        out_specs=vmem,
+        scratch_shapes=[
+            pltpu.VMEM((chips, kv_local, rows, columns), jnp.bfloat16),
+            pltpu.VMEM((chips, tall, rows), jnp.float32),
+            pltpu.VMEM((chips, kv_local, rows, columns), jnp.bfloat16),
+            pltpu.VMEM((chips, tall, rows), jnp.float32),
+            pltpu.VMEM((fars, kv_local, rows, columns), jnp.bfloat16),
+            pltpu.VMEM((fars, tall, rows), jnp.float32),
+            pltpu.SemaphoreType.DMA((2, chips * (kv_local + 1))),
+            pltpu.SemaphoreType.DMA((2, 2 * fars)),
+        ],
+        compiler_params=pltpu.CompilerParams(collective_id=1, has_side_effects=True, vmem_limit_bytes=40 * MIB),
+        name="give_back",
+    )(*parts, logs)
 
 
 def body(join_states, query_weight, out_weight, outline_keys, outline_values, branch_keys, branch_values, branch_lengths, visibility):
@@ -167,14 +282,11 @@
     for kv in range(kv_local):
         part, log = attend(gathered[kv], kv_start + kv, me, branch_lengths, visibility,
                            outline_keys, outline_values, branch_keys, branch_values)
-        parts.append(lax.all_to_all(part, "ctx", 0, 0, tiled=True).reshape(n_ctx, rows, per_kv, width))
+        parts.append(part)
         logs.append(log)
-    logs = lax.all_to_all(jnp.concatenate(logs, axis=1), "ctx", 0, 0, tiled=True).reshape(n_ctx, rows, kv_local, per_kv)
-    share = jnp.exp2(logs - jnp.max(logs, axis=0, keepdims=True))
-    share = share / jnp.sum(share, axis=0, keepdims=True)
-    mixed = [jnp.sum(share[:, :, kv, :, None] * parts[kv].astype(jnp.float32), axis=0).astype(jnp.bfloat16).reshape(rows, columns)
-             for kv in range(kv_local)]
-    mixed = jnp.concatenate(mixed, axis=1)
+    logs = jnp.concatenate(logs, axis=1)
+    logs = jnp.pad(logs, ((0, 0), (0, -head_count % 8))).reshape(n_ctx, rows, -1).transpose(0, 2, 1)
+    mixed = give_back(parts, logs, n_ctx, head_count)
     partial_out = jnp.dot(mixed, out_weight, preferred_element_type=jnp.float32)
     return lax.psum_scatter(partial_out.astype(jnp.bfloat16), "head", scatter_dimension=1, tiled=True)
 

time: 254 us -> 236 us (0.929)
  Pallas kernels: 62.8 us -> 123 us
  blocking collectives: 40.6 us -> 0 us
  local copies, waits for them, and re-layouts: 38.5 us -> 12.3 us
  other arithmetic: 9.06 us -> 3.71 us
  starting transfers between devices: 3.87 us -> 0.26 us
  waiting for transfers between devices: 76.7 us -> 73.7 us
    pallas_call x0 -> x1, Pallas kernels: none -> 55.4 us  [give_back(): pl.pallas_call(functools.partial(return_kernel, n_ctx, kv_local, heads),...]
    all_to_all x2 -> x0, blocking collectives: 40.6 us -> none  [the longest x1 29.8 us: body(): lax.all_to_all(part, 'ctx', 0, 0, tiled=True)]
    mul x7 -> x0, local copies, waits for them, and re-layouts: 19.5 us -> none  [body(): share[:, :, kv, :, None] * parts[kv].astype(jnp.float32)]
    unnamed x31 -> x17, local copies, waits for them, and re-layouts: 17.2 us -> 7.07 us
    reduce_sum x3 -> x0, other arithmetic: 6.43 us -> none  [the longest x2 6.41 us: body(): jnp.sum(share[:, :, kv, :, None] * parts[kv].astype(jnp.float32), axis=0)]
    pallas_call x2, Pallas kernels: 62.8 us -> 67.1 us  [attend(): pl.pallas_call(functools.partial(attend_kernel, per_kv, 2), out_shape=(ja...]
    all_to_all x1 -> x0, starting transfers between devices: 3.6 us -> none  [body(): lax.all_to_all(part, 'ctx', 0, 0, tiled=True)]
    all_to_all x1 -> x0, waiting for transfers between devices: 3.11 us -> none  [body(): lax.all_to_all(part, 'ctx', 0, 0, tiled=True)]
  transfers between devices with their start and end apart: 4 -> 3, of which waited for: 3 -> 2; matrix products, arithmetic and copies ran while one was open for 9% -> 1% of each run, Pallas kernels for 12% -> 14%
where the time goes in v2:
time: 236 us; the launch traced here: 238 us
  Pallas kernels  123 us (52%)
  waiting for transfers between devices  73.7 us (31%)
  between operations  13.3 us (6%)
  matrix products  12.7 us (5%)
  local copies, waits for them, and re-layouts  12.3 us (5%)
  other arithmetic  3.71 us (2%)
    pallas_call x2, Pallas kernels, attend(): pl.pallas_call(functools.partial(attend_kernel, per_kv, 2), out_shape=(ja...  67.1 us
    pallas_call x1, Pallas kernels, give_back(): pl.pallas_call(functools.partial(return_kernel, n_ctx, kv_local, heads),...  55.4 us
    reduce_scatter x1, waiting for transfers between devices, body(): lax.psum_scatter(partial_out.astype(jnp.bfloat16), 'head', scatter_dimens...  45.2 us
    all_gather x2, waiting for transfers between devices, body(): lax.all_gather(rotated.reshape(rows, columns), 'ctx', axis=0, tiled=True)  27.8 us
    unnamed x17, local copies, waits for them, and re-layouts  7.07 us
    dot_general x1, matrix products, body(): partial_out = jnp.dot(mixed, out_weight, preferred_element_type=jnp.float32)  7.05 us
    dot_general x2, matrix products, body(): jnp.dot(join_states, query_weight[:, kv * columns:(kv + 1) * columns], pr...  5.67 us
  transfers between devices with their start and end apart: 3, of which 2 were waited for; matrix products, arithmetic and copies ran while one was open for 1% of the time, Pallas kernels for 14%

profile of v2, /device:TPU:0, one launch (start us, length us, event | category | flops | bytes accessed | tf_op | source)
XLA Modules:
  0.0 238.4 jit_solution(12918260557566417790)
XLA Ops:
  6.6 1.6 copy-done
  8.1 4.4 %fusion = f32[256,512]{1,0:T(8,128)} fusion(bf16[256,4096]{1,0:T(8,128)(2,1)S(1)} %copy-done, bf16[4096,1024]{1,0:T(8,128)(2,1)} %param.10), kind=kOutput, calls=%fused_computation.1 | convolution fusion | flops 1073741824 | bytes 6815744 | tf_op jit(solution)/shard_map/dot_general | solution.py:276
  12.5 0.4 copy-done.7
  12.9 1.3 fusion.2
  14.2 0.8 copy-done.4
  15.2 1.2 reshape.34
  16.4 0.5 fusion.6
  16.9 0.6 fusion.9
  17.7 0.6 maximum_multiply_fusion.1
  18.9 1.1 fusion.4
  20.1 0.7 all-gather.5.cloned.1.call-update
  21.0 0.7 copy.15.seen_ref
  21.7 0.6 pad_add_fusion.at_ref
  22.3 0.7 pad_add_fusion.1.at_ref
  23.0 27.8 %all-gather.3.cloned.1.call-done.q_ref = bf16[2048,512]{1,0:T(8,128)(2,1)} async-done(((bf16[256,512]{1,0:T(8,128)(2,1)}), bf16[2048,512]{1,0:T(8,128)(2,1)}) %all-gather.3.cloned.1.call-update) | async-done | bytes 2097168 | tf_op jit(solution)/shard_map/all_gather | solution.py:280
  50.8 33.6 %attend.2 = (bf16[2048,512]{1,0:T(8,128)(2,1)}, f32[2048,4]{1,0:T(8,128)}) custom-call(s32[2]{0:T(128)} %pad_add_fusion.at_ref, s32[8]{0:T(128)} %lengths_ref.3, s32[64,8]{1,0:T(8,128)} %copy.15.seen_ref, bf16[2048,512]{1,0:T(8,128)(2,1)} %all-gather.3.cloned.1.call-done.q_ref, bf16[8,512,128]{2,1,0:T(8,128)(2,1)} %ok_ref.3, bf16[8,512,128]{2,1,0:T(8,128)(2,1)} %ov_ref.3, ...), custom_call_target="tpu_custom_call" | custom-call | flops 8589934592 | bytes 4194304 | tf_op jit(solution)/shard_map/attend/pallas_call | solution.py:121
  84.4 1.6 copy.17
  85.9 33.5 %attend.3 = (bf16[2048,512]{1,0:T(8,128)(2,1)}, f32[2048,4]{1,0:T(8,128)}) custom-call(s32[2]{0:T(128)} %pad_add_fusion.1.at_ref, s32[8]{0:T(128)} %lengths_ref.3, s32[64,8]{1,0:T(8,128)} %copy.15.seen_ref, bf16[2048,512]{1,0:T(8,128)(2,1)} %all-gather.5.cloned.1.call-done.q_ref, bf16[8,512,128]{2,1,0:T(8,128)(2,1)} %ok_ref.3, bf16[8,512,128]{2,1,0:T(8,128)(2,1)} %ov_ref.3, ...), custom_call_target="tpu_custom_call" | custom-call | flops 8589934592 | bytes 4194304 | tf_op jit(solution)/shard_map/attend/pallas_call | solution.py:121
  119.4 1.6 copy.18
  121.0 1.6 copy-done.1
  122.6 1.6 copy-done.2
  124.2 55.4 %give_back.1 = bf16[256,1024]{1,0:T(8,128)(2,1)S(1)} custom-call(bf16[2048,512]{1,0:T(8,128)(2,1)S(1)} %copy-done.1, bf16[2048,512]{1,0:T(8,128)(2,1)S(1)} %copy-done.2, f32[8,8,256]{2,1,0:T(8,128)S(1)} %bitcast.28), custom_call_target="tpu_custom_call" | custom-call | tf_op jit(solution)/shard_map/give_back/pallas_call | solution.py:241
  179.6 7.1 %convolution_convert_fusion = bf16[256,4096]{1,0:T(8,128)(2,1)} fusion(bf16[256,1024]{1,0:T(8,128)(2,1)S(1)} %give_back.1, bf16[1024,4096]{1,0:T(8,128)(2,1)} %param.11), kind=kOutput, calls=%fused_computation | convolution fusion | flops 2148532224 | bytes 11010048 | tf_op jit(solution)/shard_map/dot_general | solution.py:290
  186.7 45.2 %reduce-scatter.2.cloned.1.call-done = bf16[256,1024]{1,0:T(8,128)(2,1)} async-done(((bf16[256,4096]{1,0:T(8,128)(2,1)}), bf16[256,1024]{1,0:T(8,128)(2,1)}) %reduce-scatter.2.cloned.1.call-update) | async-done | bytes 524304 | tf_op jit(solution)/shard_map/reduce_scatter | solution.py:291
  (23 shorter events, 1.2 us)
Async XLA Ops:
  6.5 1.6 copy-start
  6.5 44.2 %all-gather.3.cloned.1.call-start = ((), (), s32[]{:S(2)}) async-start(), calls=%async_computation.1 | async-start | bytes 2359296 | tf_op jit(solution)/shard_map/all_gather | solution.py:280
  8.1 4.8 %copy-start.7 = (bf16[4096,1024]{1,0:T(8,128)(2,1)S(1)}, bf16[4096,1024]{1,0:T(8,128)(2,1)}, u32[]{:S(2)}) copy-start(bf16[4096,1024]{1,0:T(8,128)(2,1)} %param.10) | copy-start | bytes 25165828
  14.2 0.8 copy-start.4
  17.7 1.0 copy-start.3
  17.7 1.2 copy-start.5
  18.3 2.7 %copy-start.6 = (s32[64,8]{0,1:T(8,128)S(1)}, s32[64,8]{0,1:T(8,128)}, u32[]{:S(2)}) copy-start(s32[64,8]{0,1:T(8,128)} %param.17) | copy-start | bytes 6148
  20.0 65.9 %all-gather.5.cloned.1.call-start = ((), (), s32[]{:S(2)}) async-start(), calls=%async_computation.2 | async-start | bytes 2359296 | tf_op jit(solution)/shard_map/all_gather | solution.py:280
  20.8 211.1 %reduce-scatter.2.cloned.1.call-start = ((), (), s32[]{:S(2)}) async-start(), calls=%async_computation.3 | async-start | bytes 2621440 | tf_op jit(solution)/shard_map/reduce_scatter | solution.py:291
  121.0 1.6 copy-start.1
  122.6 1.6 copy-start.2
Sparse Core Ops, SparseCore 0:
  20.2 30.5 all-gather.2
  52.7 27.9 all-gather.4
  186.8 44.9 reduce-scatter.1

commit v3 on v2

--- a/solution.py
+++ b/solution.py
@@ -13,7 +13,7 @@
 HIDE = 1e30
 CHUNK = 512
 CHAINS = 2
-PAD = 16
+SHARES = 2
 MIB = 1 << 20
 
 
@@ -27,31 +27,31 @@
     return jnp.concatenate([cosine, cosine], axis=1), jnp.concatenate([-sine, sine], axis=1)
 
 
-def attend_kernel(per_kv, blocks_each, at_ref, lengths_ref, seen_ref, q_ref, ok_ref, ov_ref, bk_ref, bv_ref,
-                  o_ref, stat_ref, ov_turned, bv_turned, order):
+def attend_kernel(per_kv, blocks_each, share, shares, n_ctx, at_ref, lengths_ref, seen_ref, q_ref, ok_ref, ov_ref, bk_ref, bv_ref,
+                  o_ref, stat_ref, ov_wide, bv_wide, order):
     width = ok_ref.shape[2]
     me = at_ref[1]
     length = lengths_ref[me]
     blocks = q_ref.shape[0] // JSPAN
+    each = blocks // n_ctx
     branch_most = bk_ref.shape[1]
     chunk = min(CHUNK, branch_most)
-    ov_turned[:width, :] = ov_ref[0].T
-    ov_turned[width:, :] = jnp.ones((PAD, ov_ref.shape[1]), jnp.bfloat16)
-    for part in range(branch_most // chunk):
-        bv_turned[part, :width, :] = bv_ref[0, part * chunk:(part + 1) * chunk].T
-        bv_turned[part, width:, :] = jnp.ones((PAD, chunk), jnp.bfloat16)
+    ov_wide[:, :width] = ov_ref[0]
+    ov_wide[:, width:] = jnp.ones((ov_ref.shape[1], width), jnp.bfloat16)
+    bv_wide[:, :width] = bv_ref[0]
+    bv_wide[:, width:] = jnp.ones((branch_most, width), jnp.bfloat16)
 
     def place(block, ends):
         front, back = ends
-        hit = seen_ref[block, me] == 1
+        hit = seen_ref[(block // each) * (each * shares) + share * each + block % each, me] == 1
         order[jnp.where(hit, front, back)] = block
         step = hit.astype(jnp.int32)
         return front + step, back - 1 + step
 
     seen_count, _ = lax.fori_loop(0, blocks, place, (jnp.int32(0), jnp.int32(blocks - 1)))
 
-    def scores(keys, query):
-        return lax.dot_general(keys, query, (((1,), (1,)), ((), ())), preferred_element_type=jnp.float32)
+    def scores(query, keys):
+        return lax.dot_general(query, keys, (((1,), (1,)), ((), ())), preferred_element_type=jnp.float32)
 
     tile = blocks_each * JSPAN
     per_turn = CHAINS * blocks_each
@@ -59,8 +59,8 @@
     def turn(step, _):
         base = step * per_turn
         starts, queries, states, shown = [], [], [], []
-        column = lax.broadcasted_iota(jnp.int32, (1, per_kv * tile), 1)
-        slot = (column // JSPAN) % blocks_each
+        row = lax.broadcasted_iota(jnp.int32, (per_kv * tile, 1), 0)
+        slot = (row // JSPAN) % blocks_each
         for chain in range(CHAINS):
             first = base + chain * blocks_each
             at = [pl.multiple_of(order[first + j] * JSPAN, JSPAN) for j in range(blocks_each)]
@@ -70,25 +70,25 @@
                 axis=0))
             shown.append(first + slot < seen_count)
         for chain in range(CHAINS):
-            s = scores(ok_ref[0], queries[chain])
-            best = jnp.max(s, axis=0, keepdims=True)
-            weights = jnp.exp2(s - best).astype(jnp.bfloat16)
-            states += [best, jnp.dot(ov_turned[...], weights, preferred_element_type=jnp.float32)]
+            s = scores(queries[chain], ok_ref[0])
+            best = jnp.max(s, axis=1, keepdims=True)
+            weights = jnp.exp2((s - best).astype(jnp.bfloat16))
+            states += [best, jnp.dot(weights, ov_wide[...], preferred_element_type=jnp.float32)]
 
         def more(part, state):
             begin = pl.multiple_of(part * chunk, chunk)
             keys = bk_ref[0, pl.ds(begin, chunk), :]
-            values = bv_turned[part]
-            place_in = begin + lax.broadcasted_iota(jnp.int32, (chunk, 1), 0)
+            values = bv_wide[pl.ds(begin, chunk), :]
+            place_in = begin + lax.broadcasted_iota(jnp.int32, (1, chunk), 1)
             bias = jnp.where(place_in < length, 0.0, -HIDE)
             out = []
             for chain in range(CHAINS):
                 best, acc = state[2 * chain], state[2 * chain + 1]
-                s = scores(keys, queries[chain]) + bias
-                grown = jnp.maximum(best, jnp.max(s, axis=0, keepdims=True))
+                s = scores(queries[chain], keys) + bias
+                grown = jnp.maximum(best, jnp.max(s, axis=1, keepdims=True))
                 new_best = jnp.where(shown[chain], grown, best)
-                weights = jnp.exp2(s - jnp.where(shown[chain], grown, HIDE)).astype(jnp.bfloat16)
-                acc = acc * jnp.exp2(best - new_best) + jnp.dot(values, weights, preferred_element_type=jnp.float32)
+                weights = jnp.exp2((s - jnp.where(shown[chain], grown, HIDE)).astype(jnp.bfloat16))
+                acc = acc * jnp.exp2(best - new_best) + jnp.dot(weights, values, preferred_element_type=jnp.float32)
                 out += [new_best, acc]
             return tuple(out)
 
@@ -96,51 +96,51 @@
         states = lax.fori_loop(0, parts, more, tuple(states))
         for chain in range(CHAINS):
             best, acc = states[2 * chain], states[2 * chain + 1]
-            total = acc[width:width + 8]
-            part_out = (acc[:width] * (1.0 / total[:1])).T.astype(o_ref.dtype)
-            logs = jnp.concatenate([best + jnp.log2(total), jnp.zeros((width - 8, per_kv * tile), jnp.float32)], axis=0).T
+            total = acc[:, width:]
+            part_out = (acc[:, :width] / total).astype(o_ref.dtype)
+            logs = best + jnp.log2(total[:, :1])
             for h in range(per_kv):
                 for j in range(blocks_each):
                     here = (h * blocks_each + j) * JSPAN
                     rows = pl.ds(starts[chain][j], JSPAN)
                     o_ref[rows, h * width:(h + 1) * width] = part_out[here:here + JSPAN]
-                    stat_ref[rows, h:h + 1] = logs[here:here + JSPAN, :1]
+                    stat_ref[0, rows, h:h + 1] = logs[here:here + JSPAN]
         return 0
 
     lax.fori_loop(0, blocks // per_turn, turn, 0)
 
 
-def attend(query, kv, me, lengths, seen, outline_keys, outline_values, branch_keys, branch_values):
+def attend(query, share, shares, n_ctx, kv_local, kv, me, lengths, seen, outline_keys, outline_values, branch_keys, branch_values):
     rows, columns = query.shape
     width = outline_keys.shape[2]
-    per_kv = columns // width
+    per_kv = columns // (width * kv_local)
     outline_here, branch_most = outline_keys.shape[1], branch_keys.shape[1]
-    whole = lambda i, at, lens, vis: (0, 0)
-    one = lambda i, at, lens, vis: (at[0], 0, 0)
+    mine = lambda i, at, lens, vis: (0, i)
+    one = lambda i, at, lens, vis: (at[0] + i, 0, 0)
     keys_all = outline_here + branch_most // 2
     return pl.pallas_call(
-        functools.partial(attend_kernel, per_kv, 2),
-        out_shape=(jax.ShapeDtypeStruct((rows, columns), jnp.bfloat16), jax.ShapeDtypeStruct((rows, per_kv), jnp.float32)),
+        functools.partial(attend_kernel, per_kv, 2, share, shares, n_ctx),
+        out_shape=(jax.ShapeDtypeStruct((rows, columns), jnp.bfloat16), jax.ShapeDtypeStruct((kv_local, rows, per_kv), jnp.float32)),
         grid_spec=pltpu.PrefetchScalarGridSpec(
             num_scalar_prefetch=3,
-            grid=(1,),
+            grid=(kv_local,),
             in_specs=[
-                pl.BlockSpec((rows, columns), whole),
+                pl.BlockSpec((rows, per_kv * width), mine),
                 pl.BlockSpec((1, outline_here, width), one),
                 pl.BlockSpec((1, outline_here, width), one),
                 pl.BlockSpec((1, branch_most, width), one),
                 pl.BlockSpec((1, branch_most, width), one),
             ],
-            out_specs=(pl.BlockSpec((rows, columns), whole), pl.BlockSpec((rows, per_kv), whole)),
+            out_specs=(pl.BlockSpec((rows, per_kv * width), mine), pl.BlockSpec((1, rows, per_kv), lambda i, at, lens, vis: (i, 0, 0))),
             scratch_shapes=[
-                pltpu.VMEM((width + PAD, outline_here), jnp.bfloat16),
-                pltpu.VMEM((branch_most // min(CHUNK, branch_most), width + PAD, min(CHUNK, branch_most)), jnp.bfloat16),
+                pltpu.VMEM((outline_here, 2 * width), jnp.bfloat16),
+                pltpu.VMEM((branch_most, 2 * width), jnp.bfloat16),
                 pltpu.SMEM((rows // JSPAN,), jnp.int32),
             ],
         ),
         compiler_params=pltpu.CompilerParams(vmem_limit_bytes=60 * MIB),
         cost_estimate=pl.CostEstimate(
-            flops=rows * columns * keys_all * 8, bytes_accessed=4 * rows * columns, transcendentals=rows * per_kv * keys_all),
+            flops=rows * columns * keys_all * 8, bytes_accessed=4 * rows * columns, transcendentals=rows * per_kv * kv_local * keys_all),
         name="attend",
     )(jnp.stack([kv, me]).astype(jnp.int32), lengths, seen, query, outline_keys, outline_values, branch_keys, branch_values)
 
@@ -231,7 +231,7 @@
             c.wait_send()
 
 
-def give_back(parts, logs, n_ctx, heads):
+def give_back(parts, logs, n_ctx, heads, number):
     kv_local = len(parts)
     rows, columns = parts[0].shape[0] // n_ctx, parts[0].shape[1]
     chips = n_ctx // 2
@@ -253,7 +253,7 @@
             pltpu.SemaphoreType.DMA((2, chips * (kv_local + 1))),
             pltpu.SemaphoreType.DMA((2, 2 * fars)),
         ],
-        compiler_params=pltpu.CompilerParams(collective_id=1, has_side_effects=True, vmem_limit_bytes=40 * MIB),
+        compiler_params=pltpu.CompilerParams(collective_id=number, has_side_effects=True, vmem_limit_bytes=40 * MIB),
         name="give_back",
     )(*parts, logs)
 
@@ -270,25 +270,33 @@
     me = lax.axis_index("ctx")
     first = outline_keys.shape[1] * n_ctx + branch_keys.shape[1] + me * rows
     cosine, sine = rope_tables(rows, width, first, width ** (-0.5) * LOG2E)
-    columns = per_kv * width
+    shares = SHARES
+    some = rows // shares
     gathered = []
-    for kv in range(kv_local):
-        queries = jnp.dot(join_states, query_weight[:, kv * columns:(kv + 1) * columns], preferred_element_type=jnp.float32)
-        queries = queries.reshape(rows, per_kv, width)
+    for share in range(shares):
+        mine = slice(share * some, (share + 1) * some)
+        queries = jnp.dot(join_states[mine], query_weight, preferred_element_type=jnp.float32)
+        queries = queries.reshape(some, head_count, width)
         turned = jnp.concatenate([queries[..., width // 2:], queries[..., :width // 2]], axis=-1)
-        rotated = (queries * cosine[:, None, :] + turned * sine[:, None, :]).astype(jnp.bfloat16)
-        gathered.append(lax.all_gather(rotated.reshape(rows, columns), "ctx", axis=0, tiled=True))
-    parts, logs = [], []
-    for kv in range(kv_local):
-        part, log = attend(gathered[kv], kv_start + kv, me, branch_lengths, visibility,
-                           outline_keys, outline_values, branch_keys, branch_values)
-        parts.append(part)
-        logs.append(log)
-    logs = jnp.concatenate(logs, axis=1)
-    logs = jnp.pad(logs, ((0, 0), (0, -head_count % 8))).reshape(n_ctx, rows, -1).transpose(0, 2, 1)
-    mixed = give_back(parts, logs, n_ctx, head_count)
-    partial_out = jnp.dot(mixed, out_weight, preferred_element_type=jnp.float32)
-    return lax.psum_scatter(partial_out.astype(jnp.bfloat16), "head", scatter_dimension=1, tiled=True)
+        rotated = (queries * cosine[mine, None, :] + turned * sine[mine, None, :]).astype(jnp.bfloat16)
+        gathered.append(lax.all_gather(rotated.reshape(some, head_count * width), "ctx", axis=0, tiled=True))
+    outs = []
+    partial_out = None
+    for share in range(shares):
+        query = gathered[share]
+        if share > 0:
+            query, partial_out = lax.optimization_barrier((query, partial_out))
+            outs.append(lax.psum_scatter(partial_out, "head", scatter_dimension=1, tiled=True))
+        part, logs = attend(query, share, shares, n_ctx, kv_local, kv_start, me, branch_lengths, visibility,
+                            outline_keys, outline_values, branch_keys, branch_values)
+        if share > 0:
+            part, outs[-1] = lax.optimization_barrier((part, outs[-1]))
+        logs = logs.reshape(kv_local, n_ctx, some, per_kv).transpose(1, 0, 3, 2).reshape(n_ctx, head_count, some)
+        logs = jnp.pad(logs, ((0, 0), (0, -head_count % 8), (0, 0)))
+        mixed = give_back([part], logs, n_ctx, head_count, share + 1)
+        partial_out = jnp.dot(mixed, out_weight, preferred_element_type=jnp.float32).astype(jnp.bfloat16)
+    outs.append(lax.psum_scatter(partial_out, "head", scatter_dimension=1, tiled=True))
+    return jnp.concatenate(outs, axis=0)
 
 
 def solution(mesh):

time: 236 us -> 207 us (0.88); the launches traced: 238 us -> 206 us
  waiting for transfers between devices: 73.7 us -> 50.3 us
  Pallas kernels: 123 us -> 108 us
  matrix products: 12.7 us -> 20.9 us
  local copies, waits for them, and re-layouts: 12.3 us -> 7.68 us
    reduce_scatter x1 -> x2, waiting for transfers between devices: 45.2 us -> 27.1 us  [body(): lax.psum_scatter(partial_out, 'head', scatter_dimension=1, tiled=True)]
    pallas_call x2, Pallas kernels: 67.1 us -> 52.5 us  [attend(): pl.pallas_call(functools.partial(attend_kernel, per_kv, 2, share, shares,...]
    dot_general x3 -> x4, matrix products: 12.7 us -> 20.9 us  [the longest x2 11.3 us: body(): jnp.dot(mixed, out_weight, preferred_element_type=jnp.float32)]
    all_gather x2, waiting for transfers between devices: 27.8 us -> 23.2 us  [body(): lax.all_gather(rotated.reshape(some, head_count * width), 'ctx', axis=0,...]
    pallas_call x2 -> x0, local copies, waits for them, and re-layouts: 3.1 us -> none  [attend(): pl.pallas_call(functools.partial(attend_kernel, per_kv, 2), out_shape=(ja...]
    unnamed x17 -> x13, local copies, waits for them, and re-layouts: 7.07 us -> 4.11 us
    pallas_call x1 -> x2, Pallas kernels: 55.4 us -> 55.3 us  [give_back(): pl.pallas_call(functools.partial(return_kernel, n_ctx, kv_local, heads),...]
  transfers between devices with their start and end apart: 3 -> 4, of which waited for: 2 -> 2; matrix products, arithmetic and copies ran while one was open for 1% -> 8% of each run, Pallas kernels for 14% -> 38%
where the time goes in v3:
time: 207 us; the launch traced here: 206 us
  Pallas kernels  108 us (52%)
  waiting for transfers between devices  50.3 us (24%)
  matrix products  20.9 us (10%)
  between operations  13.3 us (6%)
  local copies, waits for them, and re-layouts  7.68 us (4%)
  other arithmetic  5.3 us (3%)
    pallas_call x2, Pallas kernels, give_back(): pl.pallas_call(functools.partial(return_kernel, n_ctx, kv_local, heads),...  55.3 us
    pallas_call x2, Pallas kernels, attend(): pl.pallas_call(functools.partial(attend_kernel, per_kv, 2, share, shares,...  52.5 us
    reduce_scatter x2, waiting for transfers between devices, body(): lax.psum_scatter(partial_out, 'head', scatter_dimension=1, tiled=True)  27.1 us
    all_gather x2, waiting for transfers between devices, body(): lax.all_gather(rotated.reshape(some, head_count * width), 'ctx', axis=0,...  23.2 us
    dot_general x2, matrix products, body(): jnp.dot(mixed, out_weight, preferred_element_type=jnp.float32)  11.3 us
    dot_general x2, matrix products, body(): jnp.dot(join_states[mine], query_weight, preferred_element_type=jnp.float32)  9.61 us
  transfers between devices with their start and end apart: 4, of which 2 were waited for; matrix products, arithmetic and copies ran while one was open for 8% of the time, Pallas kernels for 38%

profile of v3, /device:TPU:0, one launch (start us, length us, event | category | flops | bytes accessed | tf_op | source)
XLA Modules:
  0.0 205.6 jit_solution(1022125350125315349)
XLA Ops:
  6.6 5.0 %fusion = f32[128,1024]{1,0:T(8,128)S(1)} fusion(bf16[4096,1024]{1,0:T(8,128)(2,1)} %param.10, bf16[256,4096]{1,0:T(8,128)(2,1)} %param.9), kind=kOutput, calls=%fused_computation.2 | convolution fusion | flops 1073741824 | bytes 9961472 | tf_op jit(solution)/shard_map/dot_general | solution.py:278
  11.7 0.2 fusion.11
  11.9 0.5 fusion.6
  12.6 0.2 maximum_multiply_fusion.1
  12.8 0.9 fusion.4
  13.8 4.6 %fusion.2 = f32[128,1024]{1,0:T(8,128)S(1)} fusion(bf16[4096,1024]{1,0:T(8,128)(2,1)} %param.10, bf16[256,4096]{1,0:T(8,128)(2,1)S(1)} %copy-done.2), kind=kOutput, calls=%fused_computation.4 | convolution fusion | flops 1073741824 | bytes 9961472 | tf_op jit(solution)/shard_map/dot_general | solution.py:278
  18.7 0.2 maximum_multiply_fusion
  19.0 0.9 fusion.5
  20.0 0.7 copy.12.seen_ref
  20.7 0.6 pad_add_fusion.at_ref
  21.3 23.2 %all-gather.5.cloned.1.call-done.q_ref = bf16[1024,1024]{1,0:T(8,128)(2,1)} async-done(((bf16[128,1024]{1,0:T(8,128)(2,1)}), bf16[1024,1024]{1,0:T(8,128)(2,1)}) %all-gather.5.cloned.1.call-update) | async-done | bytes 2097168 | tf_op jit(solution)/shard_map/all_gather | solution.py:282
  44.5 26.3 %attend.2 = (bf16[1024,1024]{1,0:T(8,128)(2,1)}, f32[2,1024,4]{2,1,0:T(8,128)}) custom-call(s32[2]{0:T(128)} %pad_add_fusion.at_ref, s32[8]{0:T(128)} %lengths_ref.3, s32[64,8]{1,0:T(8,128)} %copy.12.seen_ref, bf16[1024,1024]{1,0:T(8,128)(2,1)} %all-gather.5.cloned.1.call-done.q_ref, bf16[8,512,128]{2,1,0:T(8,128)(2,1)} %ok_ref.3, ...), custom_call_target="tpu_custom_call" | custom-call | flops 8589934592 | bytes 4194304 | tf_op jit(solution)/shard_map/attend/pallas_call | solution.py:121
  70.8 1.5 copy.11
  72.3 1.6 copy-done.1
  73.9 26.6 %give_back.2 = bf16[128,1024]{1,0:T(8,128)(2,1)S(1)} custom-call(bf16[1024,1024]{1,0:T(8,128)(2,1)S(1)} %copy-done.1, f32[8,8,128]{2,1,0:T(8,128)S(1)} %bitcast.41), custom_call_target="tpu_custom_call" | custom-call | tf_op jit(solution)/shard_map/give_back/pallas_call | solution.py:241
  100.6 5.6 %convolution_convert_fusion.1 = bf16[128,4096]{1,0:T(8,128)(2,1)} fusion(bf16[128,1024]{1,0:T(8,128)(2,1)S(1)} %give_back.2, bf16[1024,4096]{1,0:T(8,128)(2,1)} %param.11), kind=kOutput, calls=%fused_computation.1 | convolution fusion | flops 1074266112 | bytes 9699328 | tf_op jit(solution)/shard_map/dot_general | solution.py:297
  106.2 0.2 reduce-scatter.5.cloned.1.call-start
  106.4 26.2 %attend.3 = (bf16[1024,1024]{1,0:T(8,128)(2,1)}, f32[2,1024,4]{2,1,0:T(8,128)}) custom-call(s32[2]{0:T(128)} %pad_add_fusion.at_ref, s32[8]{0:T(128)} %lengths_ref.3, s32[64,8]{1,0:T(8,128)} %copy.12.seen_ref, bf16[1024,1024]{1,0:T(8,128)(2,1)} %all-gather.3.cloned.1.call-done.q_ref, bf16[8,512,128]{2,1,0:T(8,128)(2,1)} %ok_ref.3, ...), custom_call_target="tpu_custom_call" | custom-call | flops 8589934592 | bytes 4194304 | tf_op jit(solution)/shard_map/attend/pallas_call | solution.py:121
  132.7 1.5 copy.13
  134.2 1.6 copy-done
  135.8 28.7 %give_back.3 = bf16[128,1024]{1,0:T(8,128)(2,1)S(1)} custom-call(bf16[1024,1024]{1,0:T(8,128)(2,1)S(1)} %copy-done, f32[8,8,128]{2,1,0:T(8,128)S(1)} %bitcast.40), custom_call_target="tpu_custom_call" | custom-call | tf_op jit(solution)/shard_map/give_back/pallas_call | solution.py:241
  164.5 5.6 %convolution_convert_fusion = bf16[128,4096]{1,0:T(8,128)(2,1)} fusion(bf16[128,1024]{1,0:T(8,128)(2,1)S(1)} %give_back.3, bf16[1024,4096]{1,0:T(8,128)(2,1)} %param.11), kind=kOutput, calls=%fused_computation | convolution fusion | flops 1074266112 | bytes 9699328 | tf_op jit(solution)/shard_map/dot_general | solution.py:297
  170.2 27.1 %reduce-scatter.5.cloned.1.call-done = bf16[128,1024]{1,0:T(8,128)(2,1)} async-done(((bf16[128,4096]{1,0:T(8,128)(2,1)}), bf16[128,1024]{1,0:T(8,128)(2,1)}) %reduce-scatter.5.cloned.1.call-update) | async-done | bytes 262160 | tf_op jit(solution)/shard_map/reduce_scatter | solution.py:298
  197.3 1.8 pad_maximum_fusion
  (25 shorter events, 0.8 us)
Async XLA Ops:
  6.5 37.9 %all-gather.5.cloned.1.call-start = ((), (), s32[]{:S(2)}) async-start(), calls=%async_computation.3 | async-start | bytes 2359296 | tf_op jit(solution)/shard_map/all_gather | solution.py:282
  11.5 2.2 %copy-start.2 = (bf16[256,4096]{1,0:T(8,128)(2,1)S(1)}, bf16[256,4096]{1,0:T(8,128)(2,1)}, u32[]{:S(2)}) copy-start(bf16[256,4096]{1,0:T(8,128)(2,1)} %param.9) | copy-start | bytes 6291460
  13.7 6.2 %copy-start.4 = (s32[64,8]{0,1:T(8,128)S(1)}, s32[64,8]{0,1:T(8,128)}, u32[]{:S(2)}) copy-start(s32[64,8]{0,1:T(8,128)} %param.17) | copy-start | bytes 6148
  13.7 92.5 %all-gather.3.cloned.1.call-start = ((), (), s32[]{:S(2)}) async-start(), calls=%async_computation.2 | async-start | bytes 2359296 | tf_op jit(solution)/shard_map/all_gather | solution.py:282
  19.9 114.3 %reduce-scatter.3.cloned.1.call-start = ((), (), s32[]{:S(2)}) async-start(), calls=%async_computation.4 | async-start | bytes 1310720 | tf_op jit(solution)/shard_map/reduce_scatter | solution.py:289
  72.3 1.6 copy-start.1
  106.2 91.1 %reduce-scatter.5.cloned.1.call-start = ((), (), s32[]{:S(2)}) async-start(), calls=%async_computation.5 | async-start | bytes 1310720 | tf_op jit(solution)/shard_map/reduce_scatter | solution.py:298
  134.2 1.6 copy-start
  135.8 61.5 %copy-start.3 = (bf16[128,1024]{1,0:T(8,128)(2,1)S(1)}, bf16[128,1024]{1,0:T(8,128)(2,1)}, u32[]{:S(2)}) copy-start(bf16[128,1024]{1,0:T(8,128)(2,1)} %reduce-scatter.3.cloned.1.call-done) | copy-start | bytes 786436
Sparse Core Ops, SparseCore 0:
  13.8 30.5 all-gather.4
  46.4 27.8 all-gather.2
  106.3 26.4 reduce-scatter.2
  170.3 26.9 reduce-scatter.4

commit v4 on v3

--- a/solution.py
+++ b/solution.py
@@ -12,7 +12,6 @@
 LOG2E = 1.4426950408889634
 HIDE = 1e30
 CHUNK = 512
-CHAINS = 2
 SHARES = 2
 MIB = 1 << 20
 
@@ -28,7 +27,7 @@
 
 
 def attend_kernel(per_kv, blocks_each, share, shares, n_ctx, at_ref, lengths_ref, seen_ref, q_ref, ok_ref, ov_ref, bk_ref, bv_ref,
-                  o_ref, stat_ref, ov_wide, bv_wide, order):
+                  o_ref, stat_ref, ok_turned, bk_turned, ov_wide, bv_wide, order):
     width = ok_ref.shape[2]
     me = at_ref[1]
     length = lengths_ref[me]
@@ -36,6 +35,9 @@
     each = blocks // n_ctx
     branch_most = bk_ref.shape[1]
     chunk = min(CHUNK, branch_most)
+    ok_turned[...] = ok_ref[0].T
+    for part in range(branch_most // chunk):
+        bk_turned[part] = bk_ref[0, part * chunk:(part + 1) * chunk].T
     ov_wide[:, :width] = ov_ref[0]
     ov_wide[:, width:] = jnp.ones((ov_ref.shape[1], width), jnp.bfloat16)
     bv_wide[:, :width] = bv_ref[0]
@@ -50,64 +52,54 @@
 
     seen_count, _ = lax.fori_loop(0, blocks, place, (jnp.int32(0), jnp.int32(blocks - 1)))
 
-    def scores(query, keys):
-        return lax.dot_general(query, keys, (((1,), (1,)), ((), ())), preferred_element_type=jnp.float32)
-
     tile = blocks_each * JSPAN
-    per_turn = CHAINS * blocks_each
+    chunks = branch_most // chunk
 
     def turn(step, _):
-        base = step * per_turn
-        starts, queries, states, shown = [], [], [], []
-        row = lax.broadcasted_iota(jnp.int32, (per_kv * tile, 1), 0)
-        slot = (row // JSPAN) % blocks_each
-        for chain in range(CHAINS):
-            first = base + chain * blocks_each
-            at = [pl.multiple_of(order[first + j] * JSPAN, JSPAN) for j in range(blocks_each)]
-            starts.append(at)
-            queries.append(jnp.concatenate(
-                [q_ref[pl.ds(at[j], JSPAN), h * width:(h + 1) * width] for h in range(per_kv) for j in range(blocks_each)],
-                axis=0))
-            shown.append(first + slot < seen_count)
-        for chain in range(CHAINS):
-            s = scores(queries[chain], ok_ref[0])
+        base = step * blocks_each
+        starts = [pl.multiple_of(order[base + j] * JSPAN, JSPAN) for j in range(blocks_each)]
+
+        def go(live):
+            query = jnp.concatenate(
+                [q_ref[pl.ds(at, JSPAN), h * width:(h + 1) * width] for h in range(per_kv) for at in starts], axis=0)
+            s = jnp.dot(query, ok_turned[...], preferred_element_type=jnp.float32)
             best = jnp.max(s, axis=1, keepdims=True)
-            weights = jnp.exp2((s - best).astype(jnp.bfloat16))
-            states += [best, jnp.dot(weights, ov_wide[...], preferred_element_type=jnp.float32)]
-
-        def more(part, state):
-            begin = pl.multiple_of(part * chunk, chunk)
-            keys = bk_ref[0, pl.ds(begin, chunk), :]
-            values = bv_wide[pl.ds(begin, chunk), :]
-            place_in = begin + lax.broadcasted_iota(jnp.int32, (1, chunk), 1)
-            bias = jnp.where(place_in < length, 0.0, -HIDE)
-            out = []
-            for chain in range(CHAINS):
-                best, acc = state[2 * chain], state[2 * chain + 1]
-                s = scores(queries[chain], keys) + bias
-                grown = jnp.maximum(best, jnp.max(s, axis=1, keepdims=True))
-                new_best = jnp.where(shown[chain], grown, best)
-                weights = jnp.exp2((s - jnp.where(shown[chain], grown, HIDE)).astype(jnp.bfloat16))
-                acc = acc * jnp.exp2(best - new_best) + jnp.dot(weights, values, preferred_element_type=jnp.float32)
-                out += [new_best, acc]
-            return tuple(out)
-
-        parts = jnp.where(base < seen_count, (length + chunk - 1) // chunk, 0)
-        states = lax.fori_loop(0, parts, more, tuple(states))
-        for chain in range(CHAINS):
-            best, acc = states[2 * chain], states[2 * chain + 1]
+            lower = best
+            found = []
+            if live > 0:
+                row = lax.broadcasted_iota(jnp.int32, (per_kv * tile, 1), 0)
+                shown = (row & (tile - 1)) < (seen_count - base) * JSPAN
+                for part in range(live):
+                    more = jnp.dot(query, bk_turned[part], preferred_element_type=jnp.float32)
+                    if part == live - 1:
+                        place_in = part * chunk + lax.broadcasted_iota(jnp.int32, (1, chunk), 1)
+                        more = more + jnp.where(place_in < length, 0.0, -HIDE)
+                    found.append(more)
+                grown = best
+                for more in found:
+                    grown = jnp.maximum(grown, jnp.max(more, axis=1, keepdims=True))
+                best = jnp.where(shown, grown, best)
+                lower = jnp.where(shown, grown, HIDE)
+            acc = jnp.dot(jnp.exp2(s - best).astype(jnp.bfloat16), ov_wide[...], preferred_element_type=jnp.float32)
+            for part, more in enumerate(found):
+                weights = jnp.exp2(more - lower).astype(jnp.bfloat16)
+                acc += jnp.dot(weights, bv_wide[part * chunk:(part + 1) * chunk], preferred_element_type=jnp.float32)
             total = acc[:, width:]
             part_out = (acc[:, :width] / total).astype(o_ref.dtype)
             logs = best + jnp.log2(total[:, :1])
             for h in range(per_kv):
                 for j in range(blocks_each):
                     here = (h * blocks_each + j) * JSPAN
-                    rows = pl.ds(starts[chain][j], JSPAN)
+                    rows = pl.ds(starts[j], JSPAN)
                     o_ref[rows, h * width:(h + 1) * width] = part_out[here:here + JSPAN]
                     stat_ref[0, rows, h:h + 1] = logs[here:here + JSPAN]
+
+        needed = jnp.where(base < seen_count, (length + chunk - 1) // chunk, 0)
+        for live in range(chunks + 1):
+            pl.when(needed == live)(functools.partial(go, live))
         return 0
 
-    lax.fori_loop(0, blocks // per_turn, turn, 0)
+    lax.fori_loop(0, blocks // blocks_each, turn, 0)
 
 
 def attend(query, share, shares, n_ctx, kv_local, kv, me, lengths, seen, outline_keys, outline_values, branch_keys, branch_values):
@@ -119,7 +111,7 @@
     one = lambda i, at, lens, vis: (at[0] + i, 0, 0)
     keys_all = outline_here + branch_most // 2
     return pl.pallas_call(
-        functools.partial(attend_kernel, per_kv, 2, share, shares, n_ctx),
+        functools.partial(attend_kernel, per_kv, 4, share, shares, n_ctx),
         out_shape=(jax.ShapeDtypeStruct((rows, columns), jnp.bfloat16), jax.ShapeDtypeStruct((kv_local, rows, per_kv), jnp.float32)),
         grid_spec=pltpu.PrefetchScalarGridSpec(
             num_scalar_prefetch=3,
@@ -133,6 +125,8 @@
             ],
             out_specs=(pl.BlockSpec((rows, per_kv * width), mine), pl.BlockSpec((1, rows, per_kv), lambda i, at, lens, vis: (i, 0, 0))),
             scratch_shapes=[
+                pltpu.VMEM((width, outline_here), jnp.bfloat16),
+                pltpu.VMEM((branch_most // min(CHUNK, branch_most), width, min(CHUNK, branch_most)), jnp.bfloat16),
                 pltpu.VMEM((outline_here, 2 * width), jnp.bfloat16),
                 pltpu.VMEM((branch_most, 2 * width), jnp.bfloat16),
                 pltpu.SMEM((rows // JSPAN,), jnp.int32),

time: 207 us -> 187 us (0.903); the launches traced: 206 us -> 188 us
  Pallas kernels: 108 us -> 89.4 us
    pallas_call x2, Pallas kernels: 55.3 us -> 36.6 us  [give_back(): pl.pallas_call(functools.partial(return_kernel, n_ctx, kv_local, heads),...]
  transfers between devices with their start and end apart: 4 -> 4, of which waited for: 2 -> 2; matrix products, arithmetic and copies ran while one was open for 8% -> 9% of each run, Pallas kernels for 38% -> 38%
where the time goes in v4:
time: 187 us; the launch traced here: 188 us
  Pallas kernels  89.4 us (48%)
  waiting for transfers between devices  51 us (27%)
  matrix products  20.9 us (11%)
  between operations  13.3 us (7%)
  local copies, waits for them, and re-layouts  7.67 us (4%)
  other arithmetic  5.3 us (3%)
    pallas_call x2, Pallas kernels, attend(): pl.pallas_call(functools.partial(attend_kernel, per_kv, 4, share, shares,...  52.8 us
    pallas_call x2, Pallas kernels, give_back(): pl.pallas_call(functools.partial(return_kernel, n_ctx, kv_local, heads),...  36.6 us
    reduce_scatter x2, waiting for transfers between devices, body(): lax.psum_scatter(partial_out, 'head', scatter_dimension=1, tiled=True)  27.9 us
    all_gather x2, waiting for transfers between devices, body(): lax.all_gather(rotated.reshape(some, head_count * width), 'ctx', axis=0,...  23 us
    dot_general x2, matrix products, body(): jnp.dot(mixed, out_weight, preferred_element_type=jnp.float32)  11.3 us
    dot_general x2, matrix products, body(): jnp.dot(join_states[mine], query_weight, preferred_element_type=jnp.float32)  9.61 us
    unnamed x13, local copies, waits for them, and re-layouts  4.09 us
  transfers between devices with their start and end apart: 4, of which 2 were waited for; matrix products, arithmetic and copies ran while one was open for 9% of the time, Pallas kernels for 38%

profile of v4, /device:TPU:0, one launch (start us, length us, event | category | flops | bytes accessed | tf_op | source)
XLA Modules:
  0.0 188.1 jit_solution(8606013639554577499)
XLA Ops:
  6.6 5.0 %fusion = f32[128,1024]{1,0:T(8,128)S(1)} fusion(bf16[4096,1024]{1,0:T(8,128)(2,1)} %param.10, bf16[256,4096]{1,0:T(8,128)(2,1)} %param.9), kind=kOutput, calls=%fused_computation.2 | convolution fusion | flops 1073741824 | bytes 9961472 | tf_op jit(solution)/shard_map/dot_general | solution.py:272
  11.9 0.5 fusion.6
  12.6 0.2 maximum_multiply_fusion.1
  12.8 0.9 fusion.4
  13.8 4.6 %fusion.2 = f32[128,1024]{1,0:T(8,128)S(1)} fusion(bf16[4096,1024]{1,0:T(8,128)(2,1)} %param.10, bf16[256,4096]{1,0:T(8,128)(2,1)S(1)} %copy-done.2), kind=kOutput, calls=%fused_computation.4 | convolution fusion | flops 1073741824 | bytes 9961472 | tf_op jit(solution)/shard_map/dot_general | solution.py:272
  18.7 0.2 maximum_multiply_fusion
  19.0 0.9 fusion.5
  19.9 0.2 reduce-scatter.3.cloned.1.call-start
  20.1 0.7 copy.12.seen_ref
  20.8 0.6 pad_add_fusion.at_ref
  21.5 23.0 %all-gather.5.cloned.1.call-done.q_ref = bf16[1024,1024]{1,0:T(8,128)(2,1)} async-done(((bf16[128,1024]{1,0:T(8,128)(2,1)}), bf16[1024,1024]{1,0:T(8,128)(2,1)}) %all-gather.5.cloned.1.call-update) | async-done | bytes 2097168 | tf_op jit(solution)/shard_map/all_gather | solution.py:276
  44.5 27.6 %attend.2 = (bf16[1024,1024]{1,0:T(8,128)(2,1)}, f32[2,1024,4]{2,1,0:T(8,128)}) custom-call(s32[2]{0:T(128)} %pad_add_fusion.at_ref, s32[8]{0:T(128)} %lengths_ref.3, s32[64,8]{1,0:T(8,128)} %copy.12.seen_ref, bf16[1024,1024]{1,0:T(8,128)(2,1)} %all-gather.5.cloned.1.call-done.q_ref, bf16[8,512,128]{2,1,0:T(8,128)(2,1)} %ok_ref.3, ...), custom_call_target="tpu_custom_call" | custom-call | flops 8589934592 | bytes 4194304 | tf_op jit(solution)/shard_map/attend/pallas_call | solution.py:113
  72.2 1.5 copy.11
  73.7 1.6 copy-done.1
  75.3 18.3 %give_back.2 = bf16[128,1024]{1,0:T(8,128)(2,1)S(1)} custom-call(bf16[1024,1024]{1,0:T(8,128)(2,1)S(1)} %copy-done.1, f32[8,8,128]{2,1,0:T(8,128)S(1)} %bitcast.41), custom_call_target="tpu_custom_call" | custom-call | tf_op jit(solution)/shard_map/give_back/pallas_call | solution.py:235
  93.6 5.6 %convolution_convert_fusion.1 = bf16[128,4096]{1,0:T(8,128)(2,1)} fusion(bf16[128,1024]{1,0:T(8,128)(2,1)S(1)} %give_back.2, bf16[1024,4096]{1,0:T(8,128)(2,1)} %param.11), kind=kOutput, calls=%fused_computation.1 | convolution fusion | flops 1074266112 | bytes 9699328 | tf_op jit(solution)/shard_map/dot_general | solution.py:291
  99.3 0.3 reduce-scatter.5.cloned.1.call-start
  99.6 25.2 %attend.3 = (bf16[1024,1024]{1,0:T(8,128)(2,1)}, f32[2,1024,4]{2,1,0:T(8,128)}) custom-call(s32[2]{0:T(128)} %pad_add_fusion.at_ref, s32[8]{0:T(128)} %lengths_ref.3, s32[64,8]{1,0:T(8,128)} %copy.12.seen_ref, bf16[1024,1024]{1,0:T(8,128)(2,1)} %all-gather.3.cloned.1.call-done.q_ref, bf16[8,512,128]{2,1,0:T(8,128)(2,1)} %ok_ref.3, ...), custom_call_target="tpu_custom_call" | custom-call | flops 8589934592 | bytes 4194304 | tf_op jit(solution)/shard_map/attend/pallas_call | solution.py:113
  124.7 1.5 copy.13
  126.3 1.6 copy-done
  127.9 18.3 %give_back.3 = bf16[128,1024]{1,0:T(8,128)(2,1)S(1)} custom-call(bf16[1024,1024]{1,0:T(8,128)(2,1)S(1)} %copy-done, f32[8,8,128]{2,1,0:T(8,128)S(1)} %bitcast.40), custom_call_target="tpu_custom_call" | custom-call | tf_op jit(solution)/shard_map/give_back/pallas_call | solution.py:235
  146.2 5.6 %convolution_convert_fusion = bf16[128,4096]{1,0:T(8,128)(2,1)} fusion(bf16[128,1024]{1,0:T(8,128)(2,1)S(1)} %give_back.3, bf16[1024,4096]{1,0:T(8,128)(2,1)} %param.11), kind=kOutput, calls=%fused_computation | convolution fusion | flops 1074266112 | bytes 9699328 | tf_op jit(solution)/shard_map/dot_general | solution.py:291
  151.9 27.9 %reduce-scatter.5.cloned.1.call-done = bf16[128,1024]{1,0:T(8,128)(2,1)} async-done(((bf16[128,4096]{1,0:T(8,128)(2,1)}), bf16[128,1024]{1,0:T(8,128)(2,1)}) %reduce-scatter.5.cloned.1.call-update) | async-done | bytes 262160 | tf_op jit(solution)/shard_map/reduce_scatter | solution.py:292
  179.8 1.8 pad_maximum_fusion
  (25 shorter events, 1.0 us)
Async XLA Ops:
  6.5 38.0 %all-gather.5.cloned.1.call-start = ((), (), s32[]{:S(2)}) async-start(), calls=%async_computation.3 | async-start | bytes 2359296 | tf_op jit(solution)/shard_map/all_gather | solution.py:276
  11.5 2.2 %copy-start.2 = (bf16[256,4096]{1,0:T(8,128)(2,1)S(1)}, bf16[256,4096]{1,0:T(8,128)(2,1)}, u32[]{:S(2)}) copy-start(bf16[256,4096]{1,0:T(8,128)(2,1)} %param.9) | copy-start | bytes 6291460
  13.7 6.4 %copy-start.4 = (s32[64,8]{0,1:T(8,128)S(1)}, s32[64,8]{0,1:T(8,128)}, u32[]{:S(2)}) copy-start(s32[64,8]{0,1:T(8,128)} %param.17) | copy-start | bytes 6148
  13.7 85.5 %all-gather.3.cloned.1.call-start = ((), (), s32[]{:S(2)}) async-start(), calls=%async_computation.2 | async-start | bytes 2359296 | tf_op jit(solution)/shard_map/all_gather | solution.py:276
  19.9 106.4 %reduce-scatter.3.cloned.1.call-start = ((), (), s32[]{:S(2)}) async-start(), calls=%async_computation.4 | async-start | bytes 1310720 | tf_op jit(solution)/shard_map/reduce_scatter | solution.py:283
  73.7 1.6 copy-start.1
  99.3 80.5 %reduce-scatter.5.cloned.1.call-start = ((), (), s32[]{:S(2)}) async-start(), calls=%async_computation.5 | async-start | bytes 1310720 | tf_op jit(solution)/shard_map/reduce_scatter | solution.py:292
  126.3 1.6 copy-start
  127.9 51.9 %copy-start.3 = (bf16[128,1024]{1,0:T(8,128)(2,1)S(1)}, bf16[128,1024]{1,0:T(8,128)(2,1)}, u32[]{:S(2)}) copy-start(bf16[128,1024]{1,0:T(8,128)(2,1)} %reduce-scatter.3.cloned.1.call-done) | copy-start | bytes 786436
Sparse Core Ops, SparseCore 0:
  13.8 30.6 all-gather.4
  46.4 27.8 all-gather.2
  99.4 26.7 reduce-scatter.2
  152.0 27.7 reduce-scatter.4

commit v5 on v4

--- a/solution.py
+++ b/solution.py
@@ -141,8 +141,8 @@
 
 def return_kernel(n_ctx, kv_local, heads, *refs):
     parts = refs[:kv_local]
-    logs_ref, mixed_ref, near, near_logs, joined, joined_logs, far, far_logs = refs[kv_local:kv_local + 8]
-    near_sems, far_sems = refs[kv_local + 8:]
+    logs_ref, mixed_ref, near, near_logs, joined, joined_logs, far, far_logs, own_part = refs[kv_local:kv_local + 9]
+    near_sems, far_sems, own_sems = refs[kv_local + 9:]
     rows, columns = near.shape[2:]
     width = kv_local * columns // heads
     per_kv = columns // width
@@ -171,6 +171,11 @@
 
     sequence = [(j + 1) % chips for j in range(chips)]
     sequence = sequence[::-1][1:] + [0] if chips > 1 else sequence
+    own_copies = {}
+    for j in sequence:
+        mine = pl.ds(pl.multiple_of((peer(j) + core) * rows, rows), rows)
+        own_copies[j] = [pltpu.make_async_copy(parts[kv].at[mine], own_part.at[j, kv], own_sems.at[j * kv_local + kv])
+                         for kv in range(kv_local)]
     near_copies = {}
     for j in sequence:
         block = peer(j) + 1 - core
@@ -178,11 +183,13 @@
         group = [copy(logs_ref.at[block], near_logs.at[j], near_sems, j * (kv_local + 1) + kv_local, sibling)]
         for kv in range(kv_local):
             group.append(copy(parts[kv].at[mine], near.at[j, kv], near_sems, j * (kv_local + 1) + kv, sibling))
-        for c in group:
+        for c in group + own_copies[j]:
             c.start()
         near_copies[j] = group
     far_copies = {}
     for j in sequence:
+        for c in own_copies[j]:
+            c.wait()
         for c in near_copies[j]:
             c.wait_recv()
         block = peer(j) + core
@@ -192,11 +199,10 @@
         total = own_share + other_share
         joined_logs[j] = top + jnp.log2(total)
         own_wide, other_wide = spread(own_share / total), spread(other_share / total)
-        mine = pl.ds(pl.multiple_of(block * rows, rows), rows)
         for kv in range(kv_local):
             for h in range(per_kv):
                 at, head = slice(h * width, (h + 1) * width), kv * per_kv + h
-                value = (parts[kv][mine, at].astype(jnp.float32) * own_wide[:, head:head + 1]
+                value = (own_part[j, kv, :, at].astype(jnp.float32) * own_wide[:, head:head + 1]
                          + near[j, kv, :, at].astype(jnp.float32) * other_wide[:, head:head + 1])
                 joined[j, kv, :, at] = value.astype(jnp.bfloat16)
         if j > 0:
@@ -235,7 +241,7 @@
     return pl.pallas_call(
         functools.partial(return_kernel, n_ctx, kv_local, heads),
         out_shape=jax.ShapeDtypeStruct((rows, kv_local * columns), jnp.bfloat16),
-        in_specs=[vmem] * (kv_local + 1),
+        in_specs=[pl.BlockSpec(memory_space=pl.ANY)] * kv_local + [vmem],
         out_specs=vmem,
         scratch_shapes=[
             pltpu.VMEM((chips, kv_local, rows, columns), jnp.bfloat16),
@@ -244,10 +250,12 @@
             pltpu.VMEM((chips, tall, rows), jnp.float32),
             pltpu.VMEM((fars, kv_local, rows, columns), jnp.bfloat16),
             pltpu.VMEM((fars, tall, rows), jnp.float32),
+            pltpu.VMEM((chips, kv_local, rows, columns), jnp.bfloat16),
             pltpu.SemaphoreType.DMA((2, chips * (kv_local + 1))),
             pltpu.SemaphoreType.DMA((2, 2 * fars)),
+            pltpu.SemaphoreType.DMA((chips * kv_local,)),
         ],
-        compiler_params=pltpu.CompilerParams(collective_id=number, has_side_effects=True, vmem_limit_bytes=40 * MIB),
+        compiler_params=pltpu.CompilerParams(collective_id=number, has_side_effects=True, vmem_limit_bytes=60 * MIB),
         name="give_back",
     )(*parts, logs)
 

time: 187 us -> 191 us (1.021)
  Pallas kernels: 89.4 us -> 95.4 us
  local copies, waits for them, and re-layouts: 7.67 us -> 5.7 us
    pallas_call x2, Pallas kernels: 36.6 us -> 42.6 us  [give_back(): pl.pallas_call(functools.partial(return_kernel, n_ctx, kv_local, heads),...]
    unnamed x13 -> x9, local copies, waits for them, and re-layouts: 4.09 us -> 0.89 us
  transfers between devices with their start and end apart: 4 -> 4, of which waited for: 2 -> 2; matrix products, arithmetic and copies ran while one was open for 9% -> 9% of each run, Pallas kernels for 38% -> 40%
where the time goes in v5:
time: 191 us
  Pallas kernels  95.4 us (50%)
  waiting for transfers between devices  49.9 us (26%)
  matrix products  21.1 us (11%)
  between operations  13.3 us (7%)
  local copies, waits for them, and re-layouts  5.7 us (3%)
  other arithmetic  5.26 us (3%)
    pallas_call x2, Pallas kernels, attend(): pl.pallas_call(functools.partial(attend_kernel, per_kv, 4, share, shares,...  52.8 us
    pallas_call x2, Pallas kernels, give_back(): pl.pallas_call(functools.partial(return_kernel, n_ctx, kv_local, heads),...  42.6 us
    reduce_scatter x2, waiting for transfers between devices, body(): lax.psum_scatter(partial_out, 'head', scatter_dimension=1, tiled=True)  26.8 us
    all_gather x2, waiting for transfers between devices, body(): lax.all_gather(rotated.reshape(some, head_count * width), 'ctx', axis=0,...  23.1 us
    dot_general x2, matrix products, body(): jnp.dot(mixed, out_weight, preferred_element_type=jnp.float32)  11.4 us
    dot_general x2, matrix products, body(): jnp.dot(join_states[mine], query_weight, preferred_element_type=jnp.float32)  9.61 us
    reshape x2, local copies, waits for them, and re-layouts, body(): logs.reshape(kv_local, n_ctx, some, per_kv).transpose(1, 0, 3, 2)  4.33 us
  transfers between devices with their start and end apart: 4, of which 2 were waited for; matrix products, arithmetic and copies ran while one was open for 9% of the time, Pallas kernels for 40%

profile of v5, /device:TPU:0, one launch (start us, length us, event | category | flops | bytes accessed | tf_op | source)
XLA Modules:
  0.0 191.1 jit_solution(6023012158314856554)
XLA Ops:
  6.6 5.0 %fusion = f32[128,1024]{1,0:T(8,128)S(1)} fusion(bf16[4096,1024]{1,0:T(8,128)(2,1)} %param.10, bf16[256,4096]{1,0:T(8,128)(2,1)} %param.9), kind=kOutput, calls=%fused_computation.2 | convolution fusion | flops 1073741824 | bytes 9961472 | tf_op jit(solution)/shard_map/dot_general | solution.py:280
  11.7 0.2 fusion.11
  11.9 0.5 fusion.6
  12.6 0.2 maximum_multiply_fusion.1
  12.8 0.9 fusion.4
  13.8 4.6 %fusion.2 = f32[128,1024]{1,0:T(8,128)S(1)} fusion(bf16[4096,1024]{1,0:T(8,128)(2,1)} %param.10, bf16[256,4096]{1,0:T(8,128)(2,1)S(1)} %copy-done), kind=kOutput, calls=%fused_computation.4 | convolution fusion | flops 1073741824 | bytes 9961472 | tf_op jit(solution)/shard_map/dot_general | solution.py:280
  18.5 0.2 fusion.12
  18.7 0.2 maximum_multiply_fusion
  19.0 0.9 fusion.5
  19.9 0.2 reduce-scatter.3.cloned.1.call-start
  20.1 0.7 copy.12.seen_ref
  20.8 0.6 pad_add_fusion.at_ref
  21.4 23.1 %all-gather.5.cloned.1.call-done.q_ref = bf16[1024,1024]{1,0:T(8,128)(2,1)} async-done(((bf16[128,1024]{1,0:T(8,128)(2,1)}), bf16[1024,1024]{1,0:T(8,128)(2,1)}) %all-gather.5.cloned.1.call-update) | async-done | bytes 2097168 | tf_op jit(solution)/shard_map/all_gather | solution.py:284
  44.5 25.2 %attend.2 = (bf16[1024,1024]{1,0:T(8,128)(2,1)}, f32[2,1024,4]{2,1,0:T(8,128)}) custom-call(s32[2]{0:T(128)} %pad_add_fusion.at_ref, s32[8]{0:T(128)} %lengths_ref.3, s32[64,8]{1,0:T(8,128)} %copy.12.seen_ref, bf16[1024,1024]{1,0:T(8,128)(2,1)} %all-gather.5.cloned.1.call-done.q_ref, bf16[8,512,128]{2,1,0:T(8,128)(2,1)} %ok_ref.3, ...), custom_call_target="tpu_custom_call" | custom-call | flops 8589934592 | bytes 4194304 | tf_op jit(solution)/shard_map/attend/pallas_call | solution.py:113
  69.8 2.2 %copy.11 = f32[2,8,128,4]{2,3,0,1:T(4,128)} copy(f32[2,8,128,4]{3,2,1,0:T(8,128)} %bitcast.49) | data formatting | bytes 65536 | tf_op jit(solution)/shard_map/reshape | solution.py:296
  71.9 22.7 %give_back.2 = bf16[128,1024]{1,0:T(8,128)(2,1)} custom-call(bf16[1024,1024]{1,0:T(8,128)(2,1)} %get-tuple-element.13.refs_0_, f32[8,8,128]{2,1,0:T(8,128)} %bitcast.51), custom_call_target="tpu_custom_call" | custom-call | tf_op jit(solution)/shard_map/give_back/pallas_call | solution.py:241
  94.7 5.7 %convolution_convert_fusion.1 = bf16[128,4096]{1,0:T(8,128)(2,1)} fusion(bf16[128,1024]{1,0:T(8,128)(2,1)} %give_back.2, bf16[1024,4096]{1,0:T(8,128)(2,1)} %param.11), kind=kOutput, calls=%fused_computation.1 | convolution fusion | flops 1074266112 | bytes 9699328 | tf_op jit(solution)/shard_map/dot_general | solution.py:299
  100.4 0.3 reduce-scatter.5.cloned.1.call-start
  100.7 27.6 %attend.3 = (bf16[1024,1024]{1,0:T(8,128)(2,1)}, f32[2,1024,4]{2,1,0:T(8,128)}) custom-call(s32[2]{0:T(128)} %pad_add_fusion.at_ref, s32[8]{0:T(128)} %lengths_ref.3, s32[64,8]{1,0:T(8,128)} %copy.12.seen_ref, bf16[1024,1024]{1,0:T(8,128)(2,1)} %all-gather.3.cloned.1.call-done.q_ref, bf16[8,512,128]{2,1,0:T(8,128)(2,1)} %ok_ref.3, ...), custom_call_target="tpu_custom_call" | custom-call | flops 8589934592 | bytes 4194304 | tf_op jit(solution)/shard_map/attend/pallas_call | solution.py:113
  128.2 2.2 %copy.13 = f32[2,8,128,4]{2,3,0,1:T(4,128)} copy(f32[2,8,128,4]{3,2,1,0:T(8,128)} %bitcast.48) | data formatting | bytes 65536 | tf_op jit(solution)/shard_map/reshape | solution.py:296
  130.4 19.8 %give_back.3 = bf16[128,1024]{1,0:T(8,128)(2,1)} custom-call(bf16[1024,1024]{1,0:T(8,128)(2,1)} %get-tuple-element.19.refs_0_, f32[8,8,128]{2,1,0:T(8,128)} %bitcast.50), custom_call_target="tpu_custom_call" | custom-call | tf_op jit(solution)/shard_map/give_back/pallas_call | solution.py:241
  150.3 5.7 %convolution_convert_fusion = bf16[128,4096]{1,0:T(8,128)(2,1)} fusion(bf16[128,1024]{1,0:T(8,128)(2,1)} %give_back.3, bf16[1024,4096]{1,0:T(8,128)(2,1)} %param.11), kind=kOutput, calls=%fused_computation | convolution fusion | flops 1074266112 | bytes 9699328 | tf_op jit(solution)/shard_map/dot_general | solution.py:299
  156.0 26.8 %reduce-scatter.5.cloned.1.call-done = bf16[128,1024]{1,0:T(8,128)(2,1)} async-done(((bf16[128,4096]{1,0:T(8,128)(2,1)}), bf16[128,1024]{1,0:T(8,128)(2,1)}) %reduce-scatter.5.cloned.1.call-update) | async-done | bytes 262160 | tf_op jit(solution)/shard_map/reduce_scatter | solution.py:300
  182.8 1.8 pad_maximum_fusion
  (21 shorter events, 0.5 us)
Async XLA Ops:
  6.5 38.0 %all-gather.5.cloned.1.call-start = ((), (), s32[]{:S(2)}) async-start(), calls=%async_computation.3 | async-start | bytes 2359296 | tf_op jit(solution)/shard_map/all_gather | solution.py:284
  11.5 2.2 %copy-start = (bf16[256,4096]{1,0:T(8,128)(2,1)S(1)}, bf16[256,4096]{1,0:T(8,128)(2,1)}, u32[]{:S(2)}) copy-start(bf16[256,4096]{1,0:T(8,128)(2,1)} %param.9) | copy-start | bytes 6291460
  13.7 6.4 %copy-start.2 = (s32[64,8]{0,1:T(8,128)S(1)}, s32[64,8]{0,1:T(8,128)}, u32[]{:S(2)}) copy-start(s32[64,8]{0,1:T(8,128)} %param.17) | copy-start | bytes 6148
  13.7 86.6 %all-gather.3.cloned.1.call-start = ((), (), s32[]{:S(2)}) async-start(), calls=%async_computation.2 | async-start | bytes 2359296 | tf_op jit(solution)/shard_map/all_gather | solution.py:284
  19.9 110.5 %reduce-scatter.3.cloned.1.call-start = ((), (), s32[]{:S(2)}) async-start(), calls=%async_computation.4 | async-start | bytes 1310720 | tf_op jit(solution)/shard_map/reduce_scatter | solution.py:291
  100.4 82.4 %reduce-scatter.5.cloned.1.call-start = ((), (), s32[]{:S(2)}) async-start(), calls=%async_computation.5 | async-start | bytes 1310720 | tf_op jit(solution)/shard_map/reduce_scatter | solution.py:300
  130.4 52.4 %copy-start.1 = (bf16[128,1024]{1,0:T(8,128)(2,1)S(1)}, bf16[128,1024]{1,0:T(8,128)(2,1)}, u32[]{:S(2)}) copy-start(bf16[128,1024]{1,0:T(8,128)(2,1)} %reduce-scatter.3.cloned.1.call-done) | copy-start | bytes 786436
Sparse Core Ops, SparseCore 0:
  13.8 30.6 all-gather.4
  46.4 27.8 all-gather.2
  100.5 26.6 reduce-scatter.2
  156.1 26.5 reduce-scatter.4

commit v6 on v4

--- a/solution.py
+++ b/solution.py
@@ -59,15 +59,15 @@
         base = step * blocks_each
         starts = [pl.multiple_of(order[base + j] * JSPAN, JSPAN) for j in range(blocks_each)]
 
-        def go(live):
+        def go_heads(live, heads):
             query = jnp.concatenate(
-                [q_ref[pl.ds(at, JSPAN), h * width:(h + 1) * width] for h in range(per_kv) for at in starts], axis=0)
+                [q_ref[pl.ds(at, JSPAN), h * width:(h + 1) * width] for h in heads for at in starts], axis=0)
             s = jnp.dot(query, ok_turned[...], preferred_element_type=jnp.float32)
             best = jnp.max(s, axis=1, keepdims=True)
             lower = best
             found = []
             if live > 0:
-                row = lax.broadcasted_iota(jnp.int32, (per_kv * tile, 1), 0)
+                row = lax.broadcasted_iota(jnp.int32, (len(heads) * tile, 1), 0)
                 shown = (row & (tile - 1)) < (seen_count - base) * JSPAN
                 for part in range(live):
                     more = jnp.dot(query, bk_turned[part], preferred_element_type=jnp.float32)
@@ -87,12 +87,17 @@
             total = acc[:, width:]
             part_out = (acc[:, :width] / total).astype(o_ref.dtype)
             logs = best + jnp.log2(total[:, :1])
-            for h in range(per_kv):
+            for h in heads:
                 for j in range(blocks_each):
-                    here = (h * blocks_each + j) * JSPAN
+                    here = ((h - heads[0]) * blocks_each + j) * JSPAN
                     rows = pl.ds(starts[j], JSPAN)
                     o_ref[rows, h * width:(h + 1) * width] = part_out[here:here + JSPAN]
                     stat_ref[0, rows, h:h + 1] = logs[here:here + JSPAN]
+
+        def go(live):
+            half = max(1, per_kv // 2)
+            for low in range(0, per_kv, half):
+                go_heads(live, range(low, min(low + half, per_kv)))
 
         needed = jnp.where(base < seen_count, (length + chunk - 1) // chunk, 0)
         for live in range(chunks + 1):

time: 187 us -> 194 us (1.037)
  Pallas kernels: 89.4 us -> 96.3 us
    pallas_call x2, Pallas kernels: 36.6 us -> 45.1 us  [give_back(): pl.pallas_call(functools.partial(return_kernel, n_ctx, kv_local, heads),...]
  transfers between devices with their start and end apart: 4 -> 4, of which waited for: 2 -> 2; matrix products, arithmetic and copies ran while one was open for 9% -> 8% of each run, Pallas kernels for 38% -> 39%
where the time goes in v6:
time: 194 us
  Pallas kernels  96.3 us (50%)
  waiting for transfers between devices  49.9 us (26%)
  matrix products  20.9 us (11%)
  between operations  13.3 us (7%)
  local copies, waits for them, and re-layouts  7.7 us (4%)
  other arithmetic  5.3 us (3%)
    pallas_call x2, Pallas kernels, attend(): pl.pallas_call(functools.partial(attend_kernel, per_kv, 4, share, shares,...  51.2 us
    pallas_call x2, Pallas kernels, give_back(): pl.pallas_call(functools.partial(return_kernel, n_ctx, kv_local, heads),...  45.1 us
    reduce_scatter x2, waiting for transfers between devices, body(): lax.psum_scatter(partial_out, 'head', scatter_dimension=1, tiled=True)  26.8 us
    all_gather x2, waiting for transfers between devices, body(): lax.all_gather(rotated.reshape(some, head_count * width), 'ctx', axis=0,...  23 us
    dot_general x2, matrix products, body(): jnp.dot(mixed, out_weight, preferred_element_type=jnp.float32)  11.3 us
    dot_general x2, matrix products, body(): jnp.dot(join_states[mine], query_weight, preferred_element_type=jnp.float32)  9.61 us
    unnamed x13, local copies, waits for them, and re-layouts  4.11 us
  transfers between devices with their start and end apart: 4, of which 2 were waited for; matrix products, arithmetic and copies ran while one was open for 8% of the time, Pallas kernels for 39%

profile of v6, /device:TPU:0, one launch (start us, length us, event | category | flops | bytes accessed | tf_op | source)
XLA Modules:
  0.0 193.9 jit_solution(10002210931933518165)
XLA Ops:
  6.6 5.0 %fusion = f32[128,1024]{1,0:T(8,128)S(1)} fusion(bf16[4096,1024]{1,0:T(8,128)(2,1)} %param.10, bf16[256,4096]{1,0:T(8,128)(2,1)} %param.9), kind=kOutput, calls=%fused_computation.2 | convolution fusion | flops 1073741824 | bytes 9961472 | tf_op jit(solution)/shard_map/dot_general | solution.py:277
  11.9 0.5 fusion.6
  12.6 0.2 maximum_multiply_fusion.1
  12.8 0.9 fusion.4
  13.8 4.6 %fusion.2 = f32[128,1024]{1,0:T(8,128)S(1)} fusion(bf16[4096,1024]{1,0:T(8,128)(2,1)} %param.10, bf16[256,4096]{1,0:T(8,128)(2,1)S(1)} %copy-done.2), kind=kOutput, calls=%fused_computation.4 | convolution fusion | flops 1073741824 | bytes 9961472 | tf_op jit(solution)/shard_map/dot_general | solution.py:277
  18.7 0.2 maximum_multiply_fusion
  19.0 0.9 fusion.5
  19.9 0.2 reduce-scatter.3.cloned.1.call-start
  20.1 0.7 copy.12.seen_ref
  20.8 0.6 pad_add_fusion.at_ref
  21.5 23.0 %all-gather.5.cloned.1.call-done.q_ref = bf16[1024,1024]{1,0:T(8,128)(2,1)} async-done(((bf16[128,1024]{1,0:T(8,128)(2,1)}), bf16[1024,1024]{1,0:T(8,128)(2,1)}) %all-gather.5.cloned.1.call-update) | async-done | bytes 2097168 | tf_op jit(solution)/shard_map/all_gather | solution.py:281
  44.5 25.1 %attend.2 = (bf16[1024,1024]{1,0:T(8,128)(2,1)}, f32[2,1024,4]{2,1,0:T(8,128)}) custom-call(s32[2]{0:T(128)} %pad_add_fusion.at_ref, s32[8]{0:T(128)} %lengths_ref.3, s32[64,8]{1,0:T(8,128)} %copy.12.seen_ref, bf16[1024,1024]{1,0:T(8,128)(2,1)} %all-gather.5.cloned.1.call-done.q_ref, bf16[8,512,128]{2,1,0:T(8,128)(2,1)} %ok_ref.3, ...), custom_call_target="tpu_custom_call" | custom-call | flops 8589934592 | bytes 4194304 | tf_op jit(solution)/shard_map/attend/pallas_call | solution.py:118
  69.6 1.6 copy.11
  71.2 1.6 copy-done.1
  72.8 23.7 %give_back.2 = bf16[128,1024]{1,0:T(8,128)(2,1)S(1)} custom-call(bf16[1024,1024]{1,0:T(8,128)(2,1)S(1)} %copy-done.1, f32[8,8,128]{2,1,0:T(8,128)S(1)} %bitcast.41), custom_call_target="tpu_custom_call" | custom-call | tf_op jit(solution)/shard_map/give_back/pallas_call | solution.py:240
  96.5 5.6 %convolution_convert_fusion.1 = bf16[128,4096]{1,0:T(8,128)(2,1)} fusion(bf16[128,1024]{1,0:T(8,128)(2,1)S(1)} %give_back.2, bf16[1024,4096]{1,0:T(8,128)(2,1)} %param.11), kind=kOutput, calls=%fused_computation.1 | convolution fusion | flops 1074266112 | bytes 9699328 | tf_op jit(solution)/shard_map/dot_general | solution.py:296
  102.1 0.3 reduce-scatter.5.cloned.1.call-start
  102.4 26.1 %attend.3 = (bf16[1024,1024]{1,0:T(8,128)(2,1)}, f32[2,1024,4]{2,1,0:T(8,128)}) custom-call(s32[2]{0:T(128)} %pad_add_fusion.at_ref, s32[8]{0:T(128)} %lengths_ref.3, s32[64,8]{1,0:T(8,128)} %copy.12.seen_ref, bf16[1024,1024]{1,0:T(8,128)(2,1)} %all-gather.3.cloned.1.call-done.q_ref, bf16[8,512,128]{2,1,0:T(8,128)(2,1)} %ok_ref.3, ...), custom_call_target="tpu_custom_call" | custom-call | flops 8589934592 | bytes 4194304 | tf_op jit(solution)/shard_map/attend/pallas_call | solution.py:118
  128.5 1.6 copy.13
  130.1 1.6 copy-done
  131.7 21.4 %give_back.3 = bf16[128,1024]{1,0:T(8,128)(2,1)S(1)} custom-call(bf16[1024,1024]{1,0:T(8,128)(2,1)S(1)} %copy-done, f32[8,8,128]{2,1,0:T(8,128)S(1)} %bitcast.40), custom_call_target="tpu_custom_call" | custom-call | tf_op jit(solution)/shard_map/give_back/pallas_call | solution.py:240
  153.1 5.6 %convolution_convert_fusion = bf16[128,4096]{1,0:T(8,128)(2,1)} fusion(bf16[128,1024]{1,0:T(8,128)(2,1)S(1)} %give_back.3, bf16[1024,4096]{1,0:T(8,128)(2,1)} %param.11), kind=kOutput, calls=%fused_computation | convolution fusion | flops 1074266112 | bytes 9699328 | tf_op jit(solution)/shard_map/dot_general | solution.py:296
  158.8 26.8 %reduce-scatter.5.cloned.1.call-done = bf16[128,1024]{1,0:T(8,128)(2,1)} async-done(((bf16[128,4096]{1,0:T(8,128)(2,1)}), bf16[128,1024]{1,0:T(8,128)(2,1)}) %reduce-scatter.5.cloned.1.call-update) | async-done | bytes 262160 | tf_op jit(solution)/shard_map/reduce_scatter | solution.py:297
  185.5 1.8 pad_maximum_fusion
  (25 shorter events, 1.0 us)
Async XLA Ops:
  6.5 38.0 %all-gather.5.cloned.1.call-start = ((), (), s32[]{:S(2)}) async-start(), calls=%async_computation.3 | async-start | bytes 2359296 | tf_op jit(solution)/shard_map/all_gather | solution.py:281
  11.5 2.2 %copy-start.2 = (bf16[256,4096]{1,0:T(8,128)(2,1)S(1)}, bf16[256,4096]{1,0:T(8,128)(2,1)}, u32[]{:S(2)}) copy-start(bf16[256,4096]{1,0:T(8,128)(2,1)} %param.9) | copy-start | bytes 6291460
  13.7 6.4 %copy-start.4 = (s32[64,8]{0,1:T(8,128)S(1)}, s32[64,8]{0,1:T(8,128)}, u32[]{:S(2)}) copy-start(s32[64,8]{0,1:T(8,128)} %param.17) | copy-start | bytes 6148
  13.7 88.4 %all-gather.3.cloned.1.call-start = ((), (), s32[]{:S(2)}) async-start(), calls=%async_computation.2 | async-start | bytes 2359296 | tf_op jit(solution)/shard_map/all_gather | solution.py:281
  19.9 110.2 %reduce-scatter.3.cloned.1.call-start = ((), (), s32[]{:S(2)}) async-start(), calls=%async_computation.4 | async-start | bytes 1310720 | tf_op jit(solution)/shard_map/reduce_scatter | solution.py:288
  71.2 1.6 copy-start.1
  102.1 83.4 %reduce-scatter.5.cloned.1.call-start = ((), (), s32[]{:S(2)}) async-start(), calls=%async_computation.5 | async-start | bytes 1310720 | tf_op jit(solution)/shard_map/reduce_scatter | solution.py:297
  130.1 1.6 copy-start
  131.7 53.9 %copy-start.3 = (bf16[128,1024]{1,0:T(8,128)(2,1)S(1)}, bf16[128,1024]{1,0:T(8,128)(2,1)}, u32[]{:S(2)}) copy-start(bf16[128,1024]{1,0:T(8,128)(2,1)} %reduce-scatter.3.cloned.1.call-done) | copy-start | bytes 786436
Sparse Core Ops, SparseCore 0:
  13.8 30.6 all-gather.4
  46.4 27.8 all-gather.2
  102.3 26.6 reduce-scatter.2
  158.9 26.5 reduce-scatter.4
